TPU v7x, 32 devices: a whole 2x2x4 slice. The times are simulated.
32 devices in a mesh: groups: 2 (over y), aux: 4 (over z), orb: 4 (over x, core).
Axes of the slice: x: 2, y: 2, z: 4, core: 2. Of those that a mesh axis runs over, the one named last changes fastest.
Arguments:
- tiles: bfloat16 [512, 128, 128], P(('groups', 'aux')), parts along dimension 0, may hold values from -0.25 to 0.25
- slot_aux: int32 [8, 64], P('groups'), parts along dimension 0, may hold values from 0 to 31
- slot_basis: int32 [8, 64], P('groups'), parts along dimension 0, may hold values from 0 to 239, as said below
- slot_count: int32 [8], P('groups'), parts along dimension 0, may hold values from 8 to 64
- orbitals: bfloat16 [61440, 2048], P(('groups', 'aux'), 'orb'), parts along dimension 0, may hold values from -6 to 6
- fit_rows: bfloat16 [8192, 4096], P(('groups', 'aux')), parts along dimension 0, may hold values from -1 to 1
Outputs:
- exchange: float32 [4096, 2048], P(('groups', 'aux'), 'orb'), parts along dimension 0
There are 2 independent parts, one for each index of `groups`. A program takes and returns all parts, laid end to end along the dimension named above; each array names one. Nothing has to cross between parts.
Inputs may be any that keep to these rules, and one draw needn't show every extreme that they name: `slot_basis`: within each row, the first slot_count entries never fall.
All inputs are finite; a program needn't handle non-finite values.
Results may differ from a plain program's by a relative error of at most 0.0031.
Values may be sent and summed in bfloat16 or wider, within the bound.
No kernel may reach another device: no remote copies, remote signals or barrier semaphores. Data moves between devices by JAX's collectives and lax.ppermute only.
A program may use at most 192 MiB of HBM per device.

v0:
```python
import jax
import jax.numpy as jnp
from jax import lax
from jax.sharding import PartitionSpec as P


def run_slots(running, panel_piece, anchor, chosen, owners, bases, row_count):
    slot_total = chosen.shape[0]
    tile_width = chosen.shape[1]
    piece_rows = panel_piece.shape[0]
    aux_blocks = running.shape[0]
    block_slots = min(32, slot_total)
    in_use = jnp.arange(slot_total, dtype=jnp.int32) < row_count
    lead_row = bases * tile_width
    first_live = jnp.sum(in_use & (lead_row + tile_width <= anchor))
    last_live = jnp.sum(in_use & (lead_row < anchor + piece_rows))
    padded = jnp.pad(panel_piece, ((tile_width, tile_width), (0, 0)))
    block_ids = jnp.arange(aux_blocks, dtype=jnp.int32)

    def one_block(counter, inner):
        first_slot = first_live + counter * block_slots
        begin_slot = jnp.minimum(first_slot, slot_total - block_slots)
        places = begin_slot + jnp.arange(block_slots, dtype=jnp.int32)
        active = (places >= first_slot) & (places < last_live)
        part_tiles = lax.dynamic_slice_in_dim(chosen, begin_slot, block_slots, 0)
        part_lead = lax.dynamic_slice_in_dim(lead_row, begin_slot, block_slots, 0)
        part_owner = lax.dynamic_slice_in_dim(owners, begin_slot, block_slots, 0)
        offset = jnp.clip(part_lead - anchor + tile_width, 0, piece_rows + tile_width)
        fetched = jax.vmap(
            lambda where_row: lax.dynamic_slice_in_dim(padded, where_row, tile_width, 0)
        )(offset)
        halfway = jnp.einsum(
            "spm,smo->spo", part_tiles, fetched, preferred_element_type=jnp.float32
        )
        selector = jnp.where(
            (block_ids[:, None] == part_owner[None, :]) & active[None, :], 1.0, 0.0
        ).astype(jnp.float32)
        added = jnp.einsum(
            "as,spo->apo",
            selector,
            halfway,
            precision=lax.Precision.HIGHEST,
            preferred_element_type=jnp.float32,
        )
        return inner + added

    steps_needed = (last_live - first_live + block_slots - 1) // block_slots
    return lax.fori_loop(0, steps_needed, one_block, running)


def shards(tiles, slot_aux, slot_basis, slot_count, orbitals, fit_rows):
    position = lax.axis_index("aux")
    tile_width = tiles.shape[1]
    aux_blocks = fit_rows.shape[1] // tile_width
    orbital_width = orbitals.shape[1]
    own_aux = lax.dynamic_index_in_dim(slot_aux, position, 0, keepdims=False)
    own_basis = lax.dynamic_index_in_dim(slot_basis, position, 0, keepdims=False)
    own_count = lax.dynamic_index_in_dim(slot_count, position, 0, keepdims=False)
    empty = jnp.zeros((aux_blocks, tile_width, orbital_width), jnp.float32)
    whole_panel = lax.all_gather(orbitals, "aux", axis=0, tiled=True)
    running = empty
    running = run_slots(running, whole_panel, 0, tiles, own_aux, own_basis, own_count)
    share_rows = (
        lax.psum_scatter(running, "aux", scatter_dimension=0, tiled=True)
        .reshape(-1, orbital_width)
        .astype(jnp.bfloat16)
    )
    columns = fit_rows
    fitted = jnp.dot(
        columns,
        lax.all_gather(share_rows, "aux", axis=0, tiled=True),
        preferred_element_type=jnp.float32,
    ).astype(jnp.bfloat16)
    wide_panel = lax.all_gather(fitted, "orb", axis=1, tiled=True)
    columns = wide_panel
    return lax.psum_scatter(
        jnp.einsum("pj,pi->ji", columns, fitted, preferred_element_type=jnp.float32),
        "aux",
        scatter_dimension=0,
        tiled=True,
    )


def solution(mesh):
    return jax.shard_map(
        shards,
        mesh=mesh,
        in_specs=(
            P(("groups", "aux"), None, None),
            P("groups", None),
            P("groups", None),
            P("groups"),
            P(("groups", "aux"), "orb"),
            P(("groups", "aux"), None),
        ),
        out_specs=P(("groups", "aux"), "orb"),
        check_vma=False,
    )
```

profile of v0, /device:TPU:13, one launch (start us, length us, event | category | flops | bytes accessed | tf_op | source)
XLA Modules:
  0.0 1155.0 jit_solution(4310965538423709495)
XLA Ops:
  11.2 523.2 %all-gather.4.cloned.1.call-done = bf16[30720,512]{1,0:T(8,128)(2,1)} async-done(((bf16[7680,512]{1,0:T(8,128)(2,1)}), bf16[30720,512]{1,0:T(8,128)(2,1)}) %all-gather.4.cloned.1.call-update) | async-done | bytes 31457296 | tf_op jit(solution)/shard_map/all_gather | solution.py:60
  534.5 21.3 %pad.5 = bf16[30976,512]{1,0:T(8,128)(2,1)} pad(bf16[30720,512]{1,0:T(8,128)(2,1)} %all-gather.4.cloned.1.call-done, bf16[]{:T(256)} %constant.64.clone.1), padding=128_128x0_0 | pad | bytes 63176704 | tf_op jit(solution)/shard_map/jit(_pad)/pad | solution.py:17
  555.8 4.4 broadcast_in_dim.17
  560.1 219.7 %while.15 = (s32[]{:T(128)}, f32[32,128,512]{2,0,1:T(8,128)}, s32[]{:T(128)}, s32[]{:T(128)}, s32[64]{0:T(128)S(1)}, /*index=5*/s32[]{:T(128)}, bf16[64,128,128]...) while((s32[]{:T(128)}, f32[32,128,512]{2,0,1:T(8,128)}, ...), condition=%wide.region_3.4_spmd.clone, body=%wide.region_2.3_spmd.clone.sunk | while | flops 1344277760 | bytes 39061936 | solution.py:48
  560.9 90.3 %while.16 = (s32[]{:T(128)}, bf16[30976,512]{1,0:T(8,128)(2,1)}, s32[32,2]{0,1:T(2,128)S(1)}, bf16[32,128,512]{2,1,0:T(8,128)(2,1)}, s32[]{:T(128)}) while((s32[]{:T(128)}, bf16[30976,512]{1,0:T(8,128)(2,1)}, s32[32,2]{0,1:T(2,128)S(1)}, bf16[32,128,512]{2,1,0:T(8,128)(2,1)}, s32[]{:T(128)}) %tuple.39), condition=%wide.while_cond, body=%wide.while_body.sunk | while | flops 2 | bytes 263257 | solution.py:30
  561.5 2.2 bitcast_dynamic-update-slice_fusion.2
  564.3 2.2 bitcast_dynamic-update-slice_fusion.2
  567.2 2.2 bitcast_dynamic-update-slice_fusion.2
  570.0 2.2 bitcast_dynamic-update-slice_fusion.2
  572.8 2.2 bitcast_dynamic-update-slice_fusion.2
  581.3 2.2 bitcast_dynamic-update-slice_fusion.2
  584.1 2.2 bitcast_dynamic-update-slice_fusion.2
  586.9 2.2 bitcast_dynamic-update-slice_fusion.2
  592.5 2.2 bitcast_dynamic-update-slice_fusion.2
  595.4 2.2 bitcast_dynamic-update-slice_fusion.2
  603.8 2.2 bitcast_dynamic-update-slice_fusion.2
  609.5 2.2 bitcast_dynamic-update-slice_fusion.2
  615.1 2.2 bitcast_dynamic-update-slice_fusion.2
  617.9 2.2 bitcast_dynamic-update-slice_fusion.2
  620.8 2.2 bitcast_dynamic-update-slice_fusion.2
  626.4 2.2 bitcast_dynamic-update-slice_fusion.2
  632.0 2.2 bitcast_dynamic-update-slice_fusion.2
  634.9 2.2 bitcast_dynamic-update-slice_fusion.2
  637.7 2.2 bitcast_dynamic-update-slice_fusion.2
  640.5 2.2 bitcast_dynamic-update-slice_fusion.2
  643.3 2.2 bitcast_dynamic-update-slice_fusion.2
  646.1 2.2 bitcast_dynamic-update-slice_fusion.2
  649.0 2.2 bitcast_dynamic-update-slice_fusion.2
  651.2 3.4 fusion.41
  655.3 14.7 %fusion.42 = f32[32,128,512]{2,0,1:T(8,128)} fusion(f32[32,128,512]{2,0,1:T(8,128)} %get-tuple-element.240, f32[32,128,512]{2,1,0:T(8,128)S(1)} %fusion.41, s32[32]{0:T(128)S(1)} %dynamic_slice.37, pred[32]{0:T(512)(128)(4,1)S(1)} %compare_and_fusion.2), kind=kOutput, calls=%fused_computation.5.clone.1 | convolution fusion | flops 807406592 | bytes 25165984 | tf_op jit(solution)/shard_map/while/body/as,spo->apo/dot_general | solution.py:38
  670.7 90.3 %while.16 = (s32[]{:T(128)}, bf16[30976,512]{1,0:T(8,128)(2,1)}, s32[32,2]{0,1:T(2,128)S(1)}, bf16[32,128,512]{2,1,0:T(8,128)(2,1)}, s32[]{:T(128)}) while((s32[]{:T(128)}, bf16[30976,512]{1,0:T(8,128)(2,1)}, s32[32,2]{0,1:T(2,128)S(1)}, bf16[32,128,512]{2,1,0:T(8,128)(2,1)}, s32[]{:T(128)}) %tuple.39), condition=%wide.while_cond, body=%wide.while_body.sunk | while | flops 2 | bytes 263257 | solution.py:30
  671.4 2.2 bitcast_dynamic-update-slice_fusion.2
  674.2 2.2 bitcast_dynamic-update-slice_fusion.2
  677.0 2.2 bitcast_dynamic-update-slice_fusion.2
  679.8 2.2 bitcast_dynamic-update-slice_fusion.2
  682.7 2.2 bitcast_dynamic-update-slice_fusion.2
  691.1 2.2 bitcast_dynamic-update-slice_fusion.2
  693.9 2.2 bitcast_dynamic-update-slice_fusion.2
  696.8 2.2 bitcast_dynamic-update-slice_fusion.2
  702.4 2.2 bitcast_dynamic-update-slice_fusion.2
  705.2 2.2 bitcast_dynamic-update-slice_fusion.2
  713.7 2.2 bitcast_dynamic-update-slice_fusion.2
  719.3 2.2 bitcast_dynamic-update-slice_fusion.2
  725.0 2.2 bitcast_dynamic-update-slice_fusion.2
  727.8 2.2 bitcast_dynamic-update-slice_fusion.2
  730.6 2.2 bitcast_dynamic-update-slice_fusion.2
  736.3 2.2 bitcast_dynamic-update-slice_fusion.2
  741.9 2.2 bitcast_dynamic-update-slice_fusion.2
  744.7 2.2 bitcast_dynamic-update-slice_fusion.2
  747.5 2.2 bitcast_dynamic-update-slice_fusion.2
  750.4 2.2 bitcast_dynamic-update-slice_fusion.2
  753.2 2.2 bitcast_dynamic-update-slice_fusion.2
  756.0 2.2 bitcast_dynamic-update-slice_fusion.2
  758.8 2.2 bitcast_dynamic-update-slice_fusion.2
  761.0 3.4 fusion.41
  765.2 14.7 %fusion.42 = f32[32,128,512]{2,0,1:T(8,128)} fusion(f32[32,128,512]{2,0,1:T(8,128)} %get-tuple-element.240, f32[32,128,512]{2,1,0:T(8,128)S(1)} %fusion.41, s32[32]{0:T(128)S(1)} %dynamic_slice.37, pred[32]{0:T(512)(128)(4,1)S(1)} %compare_and_fusion.2), kind=kOutput, calls=%fused_computation.5.clone.1 | convolution fusion | flops 807406592 | bytes 25165984 | tf_op jit(solution)/shard_map/while/body/as,spo->apo/dot_general | solution.py:38
  779.9 11.5 copy.7
  791.4 145.2 %reduce-scatter.3.cloned.1.call-done = f32[8,128,512]{2,1,0:T(8,128)} async-done(((f32[32,128,512]{2,1,0:T(8,128)}), f32[8,128,512]{2,1,0:T(8,128)}) %reduce-scatter.3.cloned.1.call-update) | async-done | bytes 2097168 | tf_op jit(solution)/shard_map/reduce_scatter | solution.py:64
  936.6 2.7 convert_element_type.22
  939.6 79.2 %all-gather.6.cloned.1.call-done = bf16[4096,512]{1,0:T(8,128)(2,1)} async-done(((bf16[1024,512]{1,0:T(8,128)(2,1)}), bf16[4096,512]{1,0:T(8,128)(2,1)}) %all-gather.6.cloned.1.call-update) | async-done | bytes 4194320 | tf_op jit(solution)/shard_map/all_gather | solution.py:71
  1018.8 10.2 convolution_convert_fusion
  1029.1 36.0 %all-gather.8.cloned.1.call-done = bf16[1024,2048]{0,1:T(8,128)(2,1)} async-done(((bf16[1024,512]{0,1:T(8,128)(2,1)}), bf16[1024,2048]{0,1:T(8,128)(2,1)}) %all-gather.8.cloned.1.call-update) | async-done | bytes 4194320 | tf_op jit(solution)/shard_map/all_gather | solution.py:74
  1065.1 6.9 fusion.23
  1071.9 76.6 %reduce-scatter.5.cloned.1.call-done = f32[512,512]{1,0:T(8,128)} async-done(((f32[2048,512]{1,0:T(8,128)}), f32[512,512]{1,0:T(8,128)}) %reduce-scatter.5.cloned.1.call-update) | async-done | bytes 1048592 | tf_op jit(solution)/shard_map/reduce_scatter | solution.py:76
  (177 shorter events, 83.7 us)
Async XLA Ops:
  6.5 4.7 copy-start
  6.5 0.8 copy-start.3
  6.5 527.9 %all-gather.4.cloned.1.call-start = ((), (), s32[]{:S(2)}) async-start(), calls=%async_computation.2 | async-start | bytes 39321600 | tf_op jit(solution)/shard_map/all_gather | solution.py:60
  7.3 929.4 %reduce-scatter.3.cloned.1.call-start = ((), (), s32[]{:S(2)}) async-start(), calls=%async_computation.3 | async-start | bytes 10485760 | tf_op jit(solution)/shard_map/reduce_scatter | solution.py:64
  555.8 4.4 copy-start.2
  791.3 227.5 %all-gather.6.cloned.1.call-start = ((), (), s32[]{:S(2)}) async-start(), calls=%async_computation.4 | async-start | bytes 5242880 | tf_op jit(solution)/shard_map/all_gather | solution.py:71
  939.4 125.7 %all-gather.8.cloned.1.call-start = ((), (), s32[]{:S(2)}) async-start(), calls=%async_computation.5 | async-start | bytes 5242880 | tf_op jit(solution)/shard_map/all_gather | solution.py:74
  1029.0 119.5 %reduce-scatter.5.cloned.1.call-start = ((), (), s32[]{:S(2)}) async-start(), calls=%async_computation.6 | async-start | bytes 5242880 | tf_op jit(solution)/shard_map/reduce_scatter | solution.py:76
  1065.1 83.4 %copy-start.1 = (s32[4,64]{1,0:T(4,128)S(1)}, s32[4,64]{1,0:T(4,128)}, u32[]{:S(2)}) copy-start(s32[4,64]{1,0:T(4,128)} %param.9) | copy-start | bytes 3076
Sparse Core Ops, SparseCore 0:
  8.9 525.4 all-gather.3
  791.5 145.1 reduce-scatter.2
  939.5 79.3 all-gather.5
  1029.1 35.8 all-gather.7
  1072.1 76.3 reduce-scatter.4
where the time goes:
time: 1160 us
  waiting for transfers between devices  861 us (74%)
  local copies, waits for them, and re-layouts  218 us (19%)
  matrix products  53.3 us (5%)
  between operations  14.4 us (1%)
    all_gather x1, waiting for transfers between devices, shards(): whole_panel = lax.all_gather(orbitals, 'aux', axis=0, tiled=True)  523 us
    gather x192, local copies, waits for them, and re-layouts  180 us
    reduce_scatter x1, waiting for transfers between devices, shards(): lax.psum_scatter(running, 'aux', scatter_dimension=0, tiled=True)  145 us
    all_gather x1, waiting for transfers between devices, shards(): lax.all_gather(share_rows, 'aux', axis=0, tiled=True)  79.2 us
    reduce_scatter x1, waiting for transfers between devices, shards(): lax.psum_scatter(jnp.einsum('pj,pi->ji', columns, fitted, preferred_eleme...  76.6 us
    all_gather x1, waiting for transfers between devices, shards(): wide_panel = lax.all_gather(fitted, 'orb', axis=1, tiled=True)  36 us
    dot_general x2, matrix products, one_block(): jnp.einsum('as,spo->apo', selector, halfway, precision=lax.Precision.HIGH...  29.4 us
  transfers between devices with their start and end apart: 5, of which 5 were waited for; matrix products, arithmetic and copies ran while one was open for 0% of the time, Pallas kernels for 0%

commit v1 on v0

v1 whole, which is shorter than its diff:
```python
import functools

import jax
import jax.numpy as jnp
from jax import lax
from jax.experimental import pallas as pl
from jax.experimental.pallas import tpu as pltpu
from jax.sharding import PartitionSpec as P

LANES = 128
CHUNKS = 16
LAG = 2


def rotation(size, by):
    return [(i, (i + by) % size) for i in range(size)]


def flipped(size, bit):
    return [(i, i ^ bit) for i in range(size)]


def spread_kernel(carry, sections, *refs):
    limits = refs[0]
    orbitals = refs[1 + 3 * len(sections)]
    sums = refs[-1]
    tile = orbitals.shape[0] and refs[3].shape[-1]
    groups = sums.shape[0]
    if carry:
        sums[...] = refs[-2][...]
    else:
        sums[...] = jnp.zeros_like(sums)
    at = 0
    for which, parts in enumerate(sections):
        owners, bases, tiles = refs[1 + 3 * which : 4 + 3 * which]

        def one(i, _, owners=owners, bases=bases, tiles=tiles):
            place = pl.multiple_of(owners[i] * tile, tile)
            panel = orbitals[pl.ds(pl.multiple_of(bases[i] * tile, tile), tile), :]
            term = jnp.dot(tiles[i], panel, preferred_element_type=jnp.float32)
            for g in range(groups):
                sums[g, pl.ds(place, tile), :] += term[:, g * LANES : (g + 1) * LANES]
            return 0

        for _ in range(parts):
            lax.fori_loop(limits[at], limits[at + 1], one, 0)
            at += 2


def spread(limits, sections, orbitals, rows, carried=None):
    width = orbitals.shape[1]
    groups = width // LANES
    vmem = pl.BlockSpec(memory_space=pltpu.VMEM)
    smem = pl.BlockSpec(memory_space=pltpu.SMEM)
    operands, specs, counts = [limits], [smem], []
    for owners, bases, tiles, parts in sections:
        operands += [owners, bases, tiles]
        specs += [smem, smem, vmem]
        counts.append(parts)
    operands.append(orbitals)
    specs.append(vmem)
    if carried is not None:
        operands.append(carried)
        specs.append(vmem)
    return pl.pallas_call(
        functools.partial(spread_kernel, carried is not None, tuple(counts)),
        out_shape=jax.ShapeDtypeStruct((groups, rows, LANES), jnp.float32),
        in_specs=specs,
        out_specs=vmem,
        compiler_params=pltpu.CompilerParams(vmem_limit_bytes=56 * 1024 * 1024),
        cost_estimate=pl.CostEstimate(
            flops=2 * 64 * 128 * 128 * width,
            bytes_accessed=24 * 1024 * 1024,
            transcendentals=0,
        ),
    )(*operands)


def all_planes(partial, planes, position):
    half = planes // 2
    total = partial.shape[0]
    size = total // CHUNKS
    rightward = [(i, i + 1) for i in range(planes - 1)]
    leftward = [(i + 1, i) for i in range(planes - 1)]
    mirrored = planes - 1 - position
    in_left = position < half
    hops = planes - 1
    steps = CHUNKS + LAG * hops
    gathered = jnp.zeros((total + LAG * (half - 1) * size, LANES), jnp.bfloat16)
    far = LAG * jnp.maximum(position, mirrored)
    got_right, got_left, paid_right, paid_left = {}, {}, {}, {}

    def own_rows(chunk):
        return lax.dynamic_slice_in_dim(partial, jnp.clip(chunk, 0, CHUNKS - 1) * size, size, 0)

    finished = []
    for s in range(steps):
        def payload(rank, on_my_half, got, paid_other):
            rows = own_rows(s - LAG * rank)
            before = got.get(s - LAG)
            if before is None:
                return rows.astype(jnp.bfloat16)
            crossing = paid_other[s - LAG]
            added = jnp.where(on_my_half, rows, jnp.where(rank == half, crossing.astype(jnp.float32), 0.0))
            return (before.astype(jnp.float32) + added).astype(jnp.bfloat16)

        right = payload(position, in_left, got_right, paid_left)
        left = payload(mirrored, ~in_left, got_left, paid_right)
        paid_right[s], paid_left[s] = right, left
        pairs_right = [(i, j) for i, j in rightward if 0 <= s - LAG * i < CHUNKS]
        pairs_left = [(i, j) for i, j in leftward if 0 <= s - LAG * (planes - 1 - i) < CHUNKS]
        if pairs_right:
            got_right[s] = lax.ppermute(right, "aux", pairs_right)
            got_left[s] = lax.ppermute(left, "aux", pairs_left)
        if s >= LAG * half:
            done = jnp.where(in_left, left, right)
            gathered = lax.dynamic_update_slice_in_dim(
                gathered, done, jnp.maximum(s - far, 0) * size, 0
            )
        finished.append(gathered)
    return finished, LAG * hops


def shards(tiles, slot_aux, slot_basis, slot_count, orbitals, fit_rows, *, groups, planes, across):
    position = lax.axis_index("aux")
    member = lax.axis_index("orb")
    slots, tile = tiles.shape[:2]
    aux_rows = fit_rows.shape[1]
    width = orbitals.shape[1]
    local_bases = orbitals.shape[0] // tile
    cap = min(slots, 2 * -(-7 * slots // (8 * planes)))
    part = cap // 2

    live = jnp.arange(slots, dtype=jnp.int32)[None, :] < slot_count[:, None]
    target = jnp.where(live, slot_basis // local_bases, planes)
    plane_ids = jnp.arange(planes, dtype=jnp.int32)
    begins = jnp.sum(target[:, None, :] < plane_ids[None, :, None], axis=2, dtype=jnp.int32)
    counts = jnp.sum(target[:, None, :] == plane_ids[None, :, None], axis=2, dtype=jnp.int32)
    away = jnp.where(plane_ids[:, None] == plane_ids[None, :], 0, counts)
    rounds = (jnp.max(away) + cap - 1) // cap
    most = rounds
    for by in range(1, groups):
        most = jnp.maximum(most, lax.ppermute(rounds, "groups", rotation(groups, by)))

    core = member % 2
    twins = flipped(across, 1)
    send_first = lax.dynamic_index_in_dim(begins, position, 0, keepdims=False)
    sources = (position - jnp.arange(1, planes, dtype=jnp.int32)) % planes
    get_first = lax.dynamic_index_in_dim(begins, position, 1, keepdims=False)[sources]
    get_count = lax.dynamic_index_in_dim(counts, position, 1, keepdims=False)[sources]

    def exchange(turn):
        mine = []
        for by in range(1, planes):
            first = send_first[(position + by) % planes] + turn * cap
            begin = jnp.minimum(first, slots - cap) + core * part
            chosen = lax.dynamic_slice_in_dim(tiles, begin, part, 0)
            mine.append(lax.ppermute(chosen, "aux", rotation(planes, by)))
        mine = jnp.concatenate(mine, axis=0)
        theirs = lax.ppermute(mine, "orb", twins)
        sections, limits = [], []
        first = get_first + turn * cap
        last = jnp.minimum(first + cap, get_first + get_count)
        for side, held in ((core, mine), (1 - core, theirs)):
            begin = jnp.minimum(first, slots - cap) + side * part
            offset = jnp.arange(planes - 1, dtype=jnp.int32) * part
            low = jnp.clip(first - begin, 0, part) + offset
            high = jnp.clip(last - begin, 0, part) + offset
            limits.append(jnp.stack([low, high], axis=1).reshape(-1))
            places = begin[:, None] + jnp.arange(part, dtype=jnp.int32)[None, :]
            owners = slot_aux[sources[:, None], places].reshape(-1)
            bases = slot_basis[sources[:, None], places].reshape(-1) - position * local_bases
            sections.append((owners, bases, held, planes - 1))
        return limits, sections

    limits, sections = exchange(jnp.int32(0))
    own_owners = lax.dynamic_index_in_dim(slot_aux, position, 0, keepdims=False)
    own_bases = lax.dynamic_index_in_dim(slot_basis, position, 0, keepdims=False) - position * local_bases
    own_first = send_first[position]
    own_last = own_first + counts[position, position]
    partial = spread(
        jnp.concatenate([jnp.stack([own_first, own_last])] + limits),
        [(own_owners, own_bases, tiles, 1)] + sections,
        orbitals,
        aux_rows,
    )

    def more(state):
        turn, sums = state
        limits, sections = exchange(turn)
        return turn + 1, spread(jnp.concatenate(limits), sections, orbitals, aux_rows, sums)

    _, partial = lax.while_loop(lambda state: state[0] < most, more, (jnp.int32(1), partial))

    finished, delay = all_planes(partial.reshape(-1, LANES), planes, position)
    column_groups = width // LANES
    square = planes == across == 4
    per_group = CHUNKS // column_groups
    fitted, pieces = [], []
    for g in range(column_groups):
        rounded = finished[(g + 1) * per_group - 1 + delay]
        rounded = lax.slice_in_dim(rounded, g * aux_rows, (g + 1) * aux_rows, axis=0)
        own = jnp.dot(fit_rows, rounded, preferred_element_type=jnp.float32).astype(jnp.bfloat16)
        fitted.append(own)
        if square:
            twin = lax.ppermute(own, "orb", flipped(across, 1))
            other = lax.ppermute(own, "orb", flipped(across, 2))
            last = lax.ppermute(other, "orb", flipped(across, 1))
            pieces.append(jnp.stack([own, twin, other, last]))
    fitted = jnp.concatenate(fitted, axis=1)
    if not square:
        wide = lax.all_gather(fitted, "orb", axis=1, tiled=True)
        partial = jnp.einsum("pj,pi->ji", wide, fitted, preferred_element_type=jnp.float32)
        return lax.psum_scatter(partial, "aux", scatter_dimension=0, tiled=True)
    pieces = jnp.concatenate(pieces, axis=2)
    blocks = jnp.einsum("dpj,pi->dji", pieces, fitted, preferred_element_type=jnp.float32)

    def block_for(plane):
        return lax.dynamic_index_in_dim(blocks, plane ^ member, 0, keepdims=False)

    result = block_for(position)
    for by in range(1, planes):
        away_block = block_for((position + by) % planes).astype(jnp.bfloat16)
        result += lax.ppermute(away_block, "aux", rotation(planes, by)).astype(jnp.float32)
    return result


def solution(mesh):
    body = functools.partial(
        shards,
        groups=mesh.shape["groups"],
        planes=mesh.shape["aux"],
        across=mesh.shape["orb"],
    )
    return jax.shard_map(
        body,
        mesh=mesh,
        in_specs=(
            P(("groups", "aux"), None, None),
            P("groups", None),
            P("groups", None),
            P("groups"),
            P(("groups", "aux"), "orb"),
            P(("groups", "aux"), None),
        ),
        out_specs=P(("groups", "aux"), "orb"),
        check_vma=False,
    )
```

time: 1160 us -> 310 us (0.27)
  waiting for transfers between devices: 861 us -> 103 us
  local copies, waits for them, and re-layouts: 218 us -> 17.6 us
  starting transfers between devices: 0.35 us -> 121 us
  matrix products: 53.3 us -> 22.4 us
  other arithmetic: 6.12 us -> 24.2 us
  Pallas kernels: 0 us -> 15.8 us
    all_gather x3 -> x0, waiting for transfers between devices: 638 us -> none  [the longest x1 523 us: shards(): whole_panel = lax.all_gather(orbitals, 'aux', axis=0, tiled=True)]
    reduce_scatter x2 -> x0, waiting for transfers between devices: 222 us -> none  [the longest x1 145 us: shards(): lax.psum_scatter(running, 'aux', scatter_dimension=0, tiled=True)]
    gather x192 -> x6, local copies, waits for them, and re-layouts: 180 us -> 6.58 us  [the longest x2 3.17 us: exchange(): owners = slot_aux[sources[:, None], places].reshape(-1)]
    ppermute x0 -> x60, starting transfers between devices: none -> 121 us  [the longest x20 57 us: all_planes(): got_right[s] = lax.ppermute(right, 'aux', pairs_right)]
    ppermute x0 -> x60, waiting for transfers between devices: none -> 103 us  [the longest x3 44.4 us: shards(): lax.ppermute(away_block, 'aux', rotation(planes, by)).astype(jnp.float32)]
    dot_general x6 -> x5, matrix products: 53.3 us -> 22.4 us  [the longest x4 18.8 us: shards(): jnp.dot(fit_rows, rounded, preferred_element_type=jnp.float32)]
    pad x1 -> x0, local copies, waits for them, and re-layouts: 21.3 us -> none  [run_slots(): padded = jnp.pad(panel_piece, ((tile_width, tile_width), (0, 0)))]
    pallas_call x0 -> x1, Pallas kernels: none -> 15.8 us  [spread(): pl.pallas_call(functools.partial(spread_kernel, carried is not None, tupl...]
  transfers between devices with their start and end apart: 5 -> 60, of which waited for: 5 -> 14; matrix products, arithmetic and copies ran while one was open for 0% -> 15% of each run, Pallas kernels for 0% -> 0%
where the time goes in v1:
time: 310 us; the launch traced here: 309 us
  starting transfers between devices  121 us (39%)
  waiting for transfers between devices  103 us (33%)
  other arithmetic  24.2 us (8%)
  matrix products  22.4 us (7%)
  local copies, waits for them, and re-layouts  17.6 us (6%)
  Pallas kernels  15.8 us (5%)
  between operations  5.51 us (2%)
    ppermute x20, starting transfers between devices, all_planes(): got_right[s] = lax.ppermute(right, 'aux', pairs_right)  57 us
    ppermute x3, waiting for transfers between devices, shards(): lax.ppermute(away_block, 'aux', rotation(planes, by)).astype(jnp.float32)  44.4 us
    ppermute x3, waiting for transfers between devices, exchange(): mine.append(lax.ppermute(chosen, 'aux', rotation(planes, by)))  36.5 us
    ppermute x20, starting transfers between devices, all_planes(): got_left[s] = lax.ppermute(left, 'aux', pairs_left)  34.1 us
    dot_general x4, matrix products, shards(): jnp.dot(fit_rows, rounded, preferred_element_type=jnp.float32)  18.8 us
    pallas_call x1, Pallas kernels, spread(): pl.pallas_call(functools.partial(spread_kernel, carried is not None, tupl...  15.8 us
    ppermute x4, starting transfers between devices, shards(): twin = lax.ppermute(own, 'orb', flipped(across, 1))  14.3 us
    ppermute x20, waiting for transfers between devices, all_planes(): got_right[s] = lax.ppermute(right, 'aux', pairs_right)  14.1 us
  transfers between devices with their start and end apart: 60, of which 14 were waited for; matrix products, arithmetic and copies ran while one was open for 15% of the time, Pallas kernels for 0%

profile of v1, /device:TPU:13, one launch (start us, length us, event | category | flops | bytes accessed | tf_op | source)
XLA Modules:
  0.0 309.3 jit_solution(783642700884000580)
XLA Ops:
  3.7 2.2 constant_dynamic-slice_fusion.3
  8.2 1.5 collective-permute-start.6
  12.1 5.3 %collective-permute-done.4 = bf16[14,128,128]{2,1,0:T(8,128)(2,1)S(1)} collective-permute-done((bf16[14,128,128]{2,1,0:T(8,128)(2,1)S(1)}, bf16[14,128,128]{2,1,0:T(8,128)(2,1)S(1)}, u32[]{:S(2)}, u32[]{:S(2)}) %collective-permute-start.4) | collective-permute-done | bytes 458784 | tf_op jit(solution)/shard_map/ppermute | solution.py:158
  17.4 28.3 %collective-permute-done.5 = bf16[14,128,128]{2,1,0:T(8,128)(2,1)S(1)} collective-permute-done((bf16[14,128,128]{2,1,0:T(8,128)(2,1)}, bf16[14,128,128]{2,1,0:T(8,128)(2,1)S(1)}, u32[]{:S(2)}, u32[]{:S(2)}) %collective-permute-start.5) | collective-permute-done | bytes 458784 | tf_op jit(solution)/shard_map/ppermute | solution.py:158
  45.8 2.9 collective-permute-done.6
  53.3 1.6 gather_fusion.6
  54.9 1.6 gather_fusion.8
  61.8 15.8 %shard_map.64 = f32[4,4096,128]{2,1,0:T(8,128)} custom-call(s32[14]{0:T(128)} %pad_add_fusion.5.refs_0_, s32[64]{0:T(128)} %get-tuple-element.485.refs_1_, s32[64]{0:T(128)} %get-tuple-element.486.refs_2_, bf16[64,128,128]{2,1,0:T(8,128)(2,1)S(1)} %copy-done.3, s32[42]{0:T(128)} %gather_fusion.6, s32[42]{0:T(128)} %get-tuple-element.488.refs_5_, ...), custom_call_target="tpu_custom_call" | custom-call | flops 1073741824 | bytes 25165824 | tf_op jit(solution)/shard_map/pallas_call | solution.py:65
  80.3 2.1 add_convert_fusion.35
  86.3 5.7 %collective-permute-done.11 = bf16[1024,128]{1,0:T(8,128)(2,1)S(1)} collective-permute-done((bf16[1024,128]{1,0:T(8,128)(2,1)S(1)}, bf16[1024,128]{1,0:T(8,128)(2,1)S(1)}, u32[]{:S(2)}, u32[]{:S(2)}) %collective-permute-start.11) | collective-permute-done | bytes 262176 | tf_op jit(solution)/shard_map/ppermute | solution.py:113
  92.0 5.6 %collective-permute-done.15 = bf16[1024,128]{1,0:T(8,128)(2,1)S(1)} collective-permute-done((bf16[1024,128]{1,0:T(8,128)(2,1)S(1)}, bf16[1024,128]{1,0:T(8,128)(2,1)S(1)}, u32[]{:S(2)}, u32[]{:S(2)}) %collective-permute-start.15) | collective-permute-done | bytes 262176 | tf_op jit(solution)/shard_map/ppermute | solution.py:113
  97.6 1.4 add_convert_fusion.34
  99.0 2.1 collective-permute-start.12
  102.6 4.0 %collective-permute-start.16 = (bf16[1024,128]{1,0:T(8,128)(2,1)S(1)}, bf16[1024,128]{1,0:T(8,128)(2,1)S(1)}, u32[]{:S(2)}, u32[]{:S(2)}) collective-permute-start(bf16[1024,128]{1,0:T(8,128)(2,1)S(1)} %get-tuple-element.458), channel_id=1, source_target_pairs={{0,4},{4,8},{1,5},{5,9},{2,6},{6,10},{3,7},{7,11},{16,20},{20,24},... | collective-permute-start | bytes 786440 | tf_op jit(solution)/shard_map/ppermute | solution.py:113
  108.4 1.8 select_dynamic-update-slice_fusion.15
  110.2 1.9 collective-permute-start.17
  112.1 3.4 %collective-permute-start.18 = (bf16[1024,128]{1,0:T(8,128)(2,1)S(1)}, bf16[1024,128]{1,0:T(8,128)(2,1)S(1)}, u32[]{:S(2)}, u32[]{:S(2)}) collective-permute-start(bf16[1024,128]{1,0:T(8,128)(2,1)S(1)} %get-tuple-element.442), channel_id=1, source_target_pairs={{0,4},{4,8},{8,12},{1,5},{5,9},{9,13},{2,6},{6,10},{10,14},{3,7},{... | collective-permute-start | bytes 786440 | tf_op jit(solution)/shard_map/ppermute | solution.py:113
  115.5 1.6 select_dynamic-update-slice_fusion.14
  117.2 1.9 collective-permute-start.19
  119.1 3.4 %collective-permute-start.20 = (bf16[1024,128]{1,0:T(8,128)(2,1)S(1)}, bf16[1024,128]{1,0:T(8,128)(2,1)S(1)}, u32[]{:S(2)}, u32[]{:S(2)}) collective-permute-start(bf16[1024,128]{1,0:T(8,128)(2,1)S(1)} %get-tuple-element.437), channel_id=1, source_target_pairs={{0,4},{4,8},{8,12},{1,5},{5,9},{9,13},{2,6},{6,10},{10,14},{3,7},{... | collective-permute-start | bytes 786440 | tf_op jit(solution)/shard_map/ppermute | solution.py:113
  122.5 1.5 select_dynamic-update-slice_fusion.13
  124.0 1.9 collective-permute-start.21
  126.0 3.3 %collective-permute-start.22 = (bf16[1024,128]{1,0:T(8,128)(2,1)S(1)}, bf16[1024,128]{1,0:T(8,128)(2,1)S(1)}, u32[]{:S(2)}, u32[]{:S(2)}) collective-permute-start(bf16[1024,128]{1,0:T(8,128)(2,1)S(1)} %get-tuple-element.434), channel_id=1, source_target_pairs={{0,4},{4,8},{8,12},{1,5},{5,9},{9,13},{2,6},{6,10},{10,14},{3,7},{... | collective-permute-start | bytes 786440 | tf_op jit(solution)/shard_map/ppermute | solution.py:113
  129.3 1.5 select_dynamic-update-slice_fusion.12
  130.8 2.0 collective-permute-start.23
  132.8 3.5 %collective-permute-start.24 = (bf16[1024,128]{1,0:T(8,128)(2,1)S(1)}, bf16[1024,128]{1,0:T(8,128)(2,1)S(1)}, u32[]{:S(2)}, u32[]{:S(2)}) collective-permute-start(bf16[1024,128]{1,0:T(8,128)(2,1)S(1)} %get-tuple-element.431), channel_id=1, source_target_pairs={{0,4},{4,8},{8,12},{1,5},{5,9},{9,13},{2,6},{6,10},{10,14},{3,7},{... | collective-permute-start | bytes 786440 | tf_op jit(solution)/shard_map/ppermute | solution.py:113
  136.6 2.0 collective-permute-start.28
  138.6 3.3 %collective-permute-start.29 = (bf16[1024,128]{1,0:T(8,128)(2,1)S(1)}, bf16[1024,128]{1,0:T(8,128)(2,1)S(1)}, u32[]{:S(2)}, u32[]{:S(2)}) collective-permute-start(bf16[1024,128]{1,0:T(8,128)(2,1)S(1)} %get-tuple-element.428), channel_id=1, source_target_pairs={{0,4},{4,8},{8,12},{1,5},{5,9},{9,13},{2,6},{6,10},{10,14},{3,7},{... | collective-permute-start | bytes 786440 | tf_op jit(solution)/shard_map/ppermute | solution.py:113
  142.2 2.0 collective-permute-start.30
  144.2 3.3 %collective-permute-start.31 = (bf16[1024,128]{1,0:T(8,128)(2,1)S(1)}, bf16[1024,128]{1,0:T(8,128)(2,1)S(1)}, u32[]{:S(2)}, u32[]{:S(2)}) collective-permute-start(bf16[1024,128]{1,0:T(8,128)(2,1)S(1)} %get-tuple-element.425), channel_id=1, source_target_pairs={{0,4},{4,8},{8,12},{1,5},{5,9},{9,13},{2,6},{6,10},{10,14},{3,7},{... | collective-permute-start | bytes 786440 | tf_op jit(solution)/shard_map/ppermute | solution.py:113
  147.5 6.5 %convolution_convert_fusion.3 = bf16[128,1024]{1,0:T(8,128)(2,1)S(1)} fusion(bf16[1024,4096]{1,0:T(8,128)(2,1)} %param.13, bf16[18432,128]{1,0:T(8,128)(2,1)S(1)} %get-tuple-element.424), kind=kOutput, calls=%fused_computation.89 | convolution fusion | flops 1073872896 | bytes 9699328 | tf_op jit(solution)/shard_map/dot_general | solution.py:203
  154.0 1.3 collective-permute-start.26
  155.6 2.0 collective-permute-start.32
  157.6 3.3 %collective-permute-start.33 = (bf16[1024,128]{1,0:T(8,128)(2,1)S(1)}, bf16[1024,128]{1,0:T(8,128)(2,1)S(1)}, u32[]{:S(2)}, u32[]{:S(2)}) collective-permute-start(bf16[1024,128]{1,0:T(8,128)(2,1)S(1)} %get-tuple-element.422), channel_id=1, source_target_pairs={{0,4},{4,8},{8,12},{1,5},{5,9},{9,13},{2,6},{6,10},{10,14},{3,7},{... | collective-permute-start | bytes 786440 | tf_op jit(solution)/shard_map/ppermute | solution.py:113
  161.2 2.0 collective-permute-start.34
  163.2 3.3 %collective-permute-start.35 = (bf16[1024,128]{1,0:T(8,128)(2,1)S(1)}, bf16[1024,128]{1,0:T(8,128)(2,1)S(1)}, u32[]{:S(2)}, u32[]{:S(2)}) collective-permute-start(bf16[1024,128]{1,0:T(8,128)(2,1)S(1)} %get-tuple-element.419), channel_id=1, source_target_pairs={{0,4},{4,8},{8,12},{1,5},{5,9},{9,13},{2,6},{6,10},{10,14},{3,7},{... | collective-permute-start | bytes 786440 | tf_op jit(solution)/shard_map/ppermute | solution.py:113
  166.8 2.0 collective-permute-start.39
  168.8 3.3 %collective-permute-start.40 = (bf16[1024,128]{1,0:T(8,128)(2,1)S(1)}, bf16[1024,128]{1,0:T(8,128)(2,1)S(1)}, u32[]{:S(2)}, u32[]{:S(2)}) collective-permute-start(bf16[1024,128]{1,0:T(8,128)(2,1)S(1)} %get-tuple-element.416), channel_id=1, source_target_pairs={{0,4},{4,8},{8,12},{1,5},{5,9},{9,13},{2,6},{6,10},{10,14},{3,7},{... | collective-permute-start | bytes 786440 | tf_op jit(solution)/shard_map/ppermute | solution.py:113
  172.4 2.9 convolution_convert_fusion.2
  175.3 2.0 collective-permute-start.41
  177.4 3.3 %collective-permute-start.42 = (bf16[1024,128]{1,0:T(8,128)(2,1)S(1)}, bf16[1024,128]{1,0:T(8,128)(2,1)S(1)}, u32[]{:S(2)}, u32[]{:S(2)}) collective-permute-start(bf16[1024,128]{1,0:T(8,128)(2,1)S(1)} %get-tuple-element.413), channel_id=1, source_target_pairs={{0,4},{4,8},{8,12},{1,5},{5,9},{9,13},{2,6},{6,10},{10,14},{3,7},{... | collective-permute-start | bytes 786440 | tf_op jit(solution)/shard_map/ppermute | solution.py:113
  180.9 2.0 collective-permute-start.43
  183.0 3.3 %collective-permute-start.44 = (bf16[1024,128]{1,0:T(8,128)(2,1)S(1)}, bf16[1024,128]{1,0:T(8,128)(2,1)S(1)}, u32[]{:S(2)}, u32[]{:S(2)}) collective-permute-start(bf16[1024,128]{1,0:T(8,128)(2,1)S(1)} %get-tuple-element.410), channel_id=1, source_target_pairs={{0,4},{4,8},{8,12},{1,5},{5,9},{9,13},{2,6},{6,10},{10,14},{3,7},{... | collective-permute-start | bytes 786440 | tf_op jit(solution)/shard_map/ppermute | solution.py:113
  187.2 1.9 collective-permute-start.45
  189.1 3.4 %collective-permute-start.46 = (bf16[1024,128]{1,0:T(8,128)(2,1)S(1)}, bf16[1024,128]{1,0:T(8,128)(2,1)S(1)}, u32[]{:S(2)}, u32[]{:S(2)}) collective-permute-start(bf16[1024,128]{1,0:T(8,128)(2,1)S(1)} %get-tuple-element.407), channel_id=1, source_target_pairs={{0,4},{4,8},{8,12},{1,5},{5,9},{9,13},{2,6},{6,10},{10,14},{3,7},{... | collective-permute-start | bytes 786440 | tf_op jit(solution)/shard_map/ppermute | solution.py:113
  192.8 1.9 collective-permute-start.50
  194.8 3.4 %collective-permute-start.51 = (bf16[1024,128]{1,0:T(8,128)(2,1)S(1)}, bf16[1024,128]{1,0:T(8,128)(2,1)S(1)}, u32[]{:S(2)}, u32[]{:S(2)}) collective-permute-start(bf16[1024,128]{1,0:T(8,128)(2,1)S(1)} %get-tuple-element.404), channel_id=1, source_target_pairs={{4,8},{8,12},{5,9},{9,13},{6,10},{10,14},{7,11},{11,15},{20,24},{2... | collective-permute-start | bytes 786440 | tf_op jit(solution)/shard_map/ppermute | solution.py:113
  198.5 2.9 convolution_convert_fusion.1
  201.3 1.9 collective-permute-start.52
  203.3 3.4 %collective-permute-start.53 = (bf16[1024,128]{1,0:T(8,128)(2,1)S(1)}, bf16[1024,128]{1,0:T(8,128)(2,1)S(1)}, u32[]{:S(2)}, u32[]{:S(2)}) collective-permute-start(bf16[1024,128]{1,0:T(8,128)(2,1)S(1)} %get-tuple-element.401), channel_id=1, source_target_pairs={{4,8},{8,12},{5,9},{9,13},{6,10},{10,14},{7,11},{11,15},{20,24},{2... | collective-permute-start | bytes 786440 | tf_op jit(solution)/shard_map/ppermute | solution.py:113
  207.0 1.3 collective-permute-start.54
  210.2 2.2 copy-done.4
  212.4 1.4 collective-permute-start.56
  214.7 13.4 %collective-permute-start.25 = (bf16[1024,128]{0,1:T(8,128)(2,1)S(1)}, bf16[1024,128]{0,1:T(8,128)(2,1)S(1)}, u32[]{:S(2)}, u32[]{:S(2)}) collective-permute-start(bf16[1024,128]{0,1:T(8,128)(2,1)S(1)} %bitcast.176), channel_id=1, source_target_pairs={{0,1},{1,0},{2,3},{3,2},{4,5},{5,4},{6,7},{7,6},{8,9},{9,8},{10,11... | collective-permute-start | bytes 786440 | tf_op jit(solution)/shard_map/ppermute | solution.py:206
  228.5 2.1 fusion.66
  232.6 2.1 fusion.68
  234.7 6.6 %convolution_convert_fusion = bf16[128,1024]{1,0:T(8,128)(2,1)S(1)} fusion(bf16[1024,4096]{1,0:T(8,128)(2,1)} %param.13, bf16[18432,128]{1,0:T(8,128)(2,1)} %fusion.68), kind=kOutput, calls=%fused_computation.86 | convolution fusion | flops 1073872896 | bytes 9699328 | tf_op jit(solution)/shard_map/dot_general | solution.py:203
  242.8 6.1 %collective-permute-done.59 = bf16[1024,128]{0,1:T(8,128)(2,1)S(1)} collective-permute-done((bf16[1024,128]{0,1:T(8,128)(2,1)S(1)}, bf16[1024,128]{0,1:T(8,128)(2,1)S(1)}, u32[]{:S(2)}, u32[]{:S(2)}) %collective-permute-start.59) | collective-permute-done | bytes 262176 | tf_op jit(solution)/shard_map/ppermute | solution.py:207
  251.4 3.5 %fusion.18 = f32[4,512,512]{2,1,0:T(8,128)S(1)} fusion(bf16[1,1024,128]{1,2,0:T(8,128)(2,1)} %bitcast.33, bf16[1,1024,128]{1,2,0:T(8,128)(2,1)S(1)} %bitcast.196, bf16[1,1024,128]{1,2,0:T(8,128)(2,1)S(1)} %bitcast.200, bf16[1,1024,128]{1,2,0:T(8,128)(2,1)S(1)} %bitcast.190, bf16[1,1024,128]{1,2,0:T(8,128)(2,1)S(1)} %bitcast.199, ...), kind=kOutput, calls=%fused_computation.54 | convolution fusion | flops 2218786816 | bytes 9437184 | tf_op jit(solution)/shard_map/dpj,pi->dji/dot_general | solution.py:216
  254.9 2.0 copy-done.6
  257.2 4.1 %collective-permute-start.61 = (bf16[512,512]{1,0:T(8,128)(2,1)S(1)}, bf16[512,512]{1,0:T(8,128)(2,1)S(1)}, u32[]{:S(2)}, u32[]{:S(2)}) collective-permute-start(bf16[512,512]{1,0:T(8,128)(2,1)S(1)} %get-tuple-element.464), channel_id=1, source_target_pairs={{0,4},{4,8},{8,12},{12,0},{1,5},{5,9},{9,13},{13,1},{2,6},{6,10},{... | collective-permute-start | bytes 1572872 | tf_op jit(solution)/shard_map/ppermute | solution.py:224
  262.5 32.1 %collective-permute-done.61 = bf16[512,512]{1,0:T(8,128)(2,1)S(1)} collective-permute-done((bf16[512,512]{1,0:T(8,128)(2,1)S(1)}, bf16[512,512]{1,0:T(8,128)(2,1)S(1)}, u32[]{:S(2)}, u32[]{:S(2)}) %collective-permute-start.61) | collective-permute-done | bytes 524320 | tf_op jit(solution)/shard_map/ppermute | solution.py:224
  294.6 11.2 %collective-permute-done.62 = bf16[512,512]{1,0:T(8,128)(2,1)S(1)} collective-permute-done((bf16[512,512]{1,0:T(8,128)(2,1)S(1)}, bf16[512,512]{1,0:T(8,128)(2,1)S(1)}, u32[]{:S(2)}, u32[]{:S(2)}) %collective-permute-start.62) | collective-permute-done | bytes 524320 | tf_op jit(solution)/shard_map/ppermute | solution.py:224
  306.9 2.5 fusion.61
  (144 shorter events, 38.9 us)
Async XLA Ops:
  0.0 51.1 %copy-start = (s32[4,64]{1,0:T(4,128)S(1)}, s32[4,64]{1,0:T(4,128)}, u32[]{:S(2)}) copy-start(s32[4,64]{1,0:T(4,128)} %param.10) | copy-start | bytes 3076
  3.7 49.7 %copy-start.1 = (s32[4,64]{1,0:T(4,128)S(1)}, s32[4,64]{1,0:T(4,128)}, u32[]{:S(2)}) copy-start(s32[4,64]{1,0:T(4,128)} %param.9) | copy-start | bytes 3076
  5.9 11.5 %collective-permute-start.4 = (bf16[14,128,128]{2,1,0:T(8,128)(2,1)S(1)}, bf16[14,128,128]{2,1,0:T(8,128)(2,1)S(1)}, u32[]{:S(2)}, u32[]{:S(2)}) collective-permute-start(bf16[14,128,128]{2,1,0:T(8,128)(2,1)S(1)} %get-tuple-element.469), channel_id=1, source_target_pairs={{0,4},{4,8},{8,12},{12,0},{1,5},{5,9},{9,13},{13,1},{2,6},{6,10},{... | collective-permute-start | bytes 1376264 | tf_op jit(solution)/shard_map/ppermute | solution.py:158
  7.1 38.6 %collective-permute-start.5 = (bf16[14,128,128]{2,1,0:T(8,128)(2,1)}, bf16[14,128,128]{2,1,0:T(8,128)(2,1)S(1)}, u32[]{:S(2)}, u32[]{:S(2)}) collective-permute-start(bf16[14,128,128]{2,1,0:T(8,128)(2,1)} %get-tuple-element.468), channel_id=1, source_target_pairs={{0,8},{4,12},{8,0},{12,4},{1,9},{5,13},{9,1},{13,5},{2,10},{6,14},... | collective-permute-start | bytes 1376264 | tf_op jit(solution)/shard_map/ppermute | solution.py:158
  8.2 40.5 %collective-permute-start.6 = (bf16[14,128,128]{2,1,0:T(8,128)(2,1)S(1)}, bf16[14,128,128]{2,1,0:T(8,128)(2,1)S(1)}, u32[]{:S(2)}, u32[]{:S(2)}) collective-permute-start(bf16[14,128,128]{2,1,0:T(8,128)(2,1)S(1)} %get-tuple-element.467), channel_id=1, source_target_pairs={{0,12},{4,0},{8,4},{12,8},{1,13},{5,1},{9,5},{13,9},{2,14},{6,2},{... | collective-permute-start | bytes 1376264 | tf_op jit(solution)/shard_map/ppermute | solution.py:158
  11.1 50.0 %collective-permute-start.8 = (s32[]{:T(128)}, s32[]{:T(128)}, u32[]{:S(2)}, u32[]{:S(2)}) collective-permute-start(s32[]{:T(128)} %select_n.854), channel_id=1, source_target_pairs={{0,16},{16,0},{1,17},{17,1},{2,18},{18,2},{3,19},{19,3},{4,20},{20... | collective-permute-start | bytes 20 | tf_op jit(solution)/shard_map/ppermute | solution.py:143
  48.7 13.0 %collective-permute-start.7 = (bf16[42,128,128]{2,1,0:T(8,128)(2,1)S(1)}, bf16[42,128,128]{2,1,0:T(8,128)(2,1)}, u32[]{:S(2)}, u32[]{:S(2)}) collective-permute-start(bf16[42,128,128]{2,1,0:T(8,128)(2,1)S(1)} %constant_dynamic-update-slice_fusion.3.refs_6_), channel_id=1, source_target_pairs={{0,1},{1,0},{2,3},{3,2},{4,5},{5,4},{6,7},{7,6},{8,9},{9,8},{10,11... | collective-permute-start | bytes 4128776 | tf_op jit(solution)/shard_map/ppermute | solution.py:160
  78.9 1.4 collective-permute-start.13
  79.6 0.7 collective-permute-start.9
  82.4 9.6 %collective-permute-start.11 = (bf16[1024,128]{1,0:T(8,128)(2,1)S(1)}, bf16[1024,128]{1,0:T(8,128)(2,1)S(1)}, u32[]{:S(2)}, u32[]{:S(2)}) collective-permute-start(bf16[1024,128]{1,0:T(8,128)(2,1)S(1)} %get-tuple-element.461), channel_id=1, source_target_pairs={{0,4},{1,5},{2,6},{3,7},{16,20},{17,21},{18,22},{19,23}} | collective-permute-start | bytes 786440 | tf_op jit(solution)/shard_map/ppermute | solution.py:113
  83.7 14.0 %collective-permute-start.15 = (bf16[1024,128]{1,0:T(8,128)(2,1)S(1)}, bf16[1024,128]{1,0:T(8,128)(2,1)S(1)}, u32[]{:S(2)}, u32[]{:S(2)}) collective-permute-start(bf16[1024,128]{1,0:T(8,128)(2,1)S(1)} %get-tuple-element.440), channel_id=1, source_target_pairs={{0,4},{1,5},{2,6},{3,7},{16,20},{17,21},{18,22},{19,23}} | collective-permute-start | bytes 786440 | tf_op jit(solution)/shard_map/ppermute | solution.py:113
  85.0 21.6 %collective-permute-start.10 = (bf16[1024,128]{1,0:T(8,128)(2,1)S(1)}, bf16[1024,128]{1,0:T(8,128)(2,1)S(1)}, u32[]{:S(2)}, u32[]{:S(2)}) collective-permute-start(bf16[1024,128]{1,0:T(8,128)(2,1)S(1)} %get-tuple-element.460), channel_id=1, source_target_pairs={{8,4},{12,8},{9,5},{13,9},{10,6},{14,10},{11,7},{15,11},{24,20},{2... | collective-permute-start | bytes 786440 | tf_op jit(solution)/shard_map/ppermute | solution.py:114
  99.0 8.7 %collective-permute-start.12 = (bf16[1024,128]{1,0:T(8,128)(2,1)S(1)}, bf16[1024,128]{1,0:T(8,128)(2,1)S(1)}, u32[]{:S(2)}, u32[]{:S(2)}) collective-permute-start(bf16[1024,128]{1,0:T(8,128)(2,1)S(1)} %get-tuple-element.459), channel_id=1, source_target_pairs={{0,4},{4,8},{1,5},{5,9},{2,6},{6,10},{3,7},{7,11},{16,20},{20,24},... | collective-permute-start | bytes 786440 | tf_op jit(solution)/shard_map/ppermute | solution.py:113
  101.3 14.2 %collective-permute-start.14 = (bf16[1024,128]{1,0:T(8,128)(2,1)S(1)}, bf16[1024,128]{1,0:T(8,128)(2,1)S(1)}, u32[]{:S(2)}, u32[]{:S(2)}) collective-permute-start(bf16[1024,128]{1,0:T(8,128)(2,1)S(1)} %get-tuple-element.439), channel_id=1, source_target_pairs={{8,4},{12,8},{9,5},{13,9},{10,6},{14,10},{11,7},{15,11},{24,20},{2... | collective-permute-start | bytes 786440 | tf_op jit(solution)/shard_map/ppermute | solution.py:114
  102.6 12.9 %collective-permute-start.16 = (bf16[1024,128]{1,0:T(8,128)(2,1)S(1)}, bf16[1024,128]{1,0:T(8,128)(2,1)S(1)}, u32[]{:S(2)}, u32[]{:S(2)}) collective-permute-start(bf16[1024,128]{1,0:T(8,128)(2,1)S(1)} %get-tuple-element.458), channel_id=1, source_target_pairs={{0,4},{4,8},{1,5},{5,9},{2,6},{6,10},{3,7},{7,11},{16,20},{20,24},... | collective-permute-start | bytes 786440 | tf_op jit(solution)/shard_map/ppermute | solution.py:113
  107.8 28.6 %slice-start = ((s8[8388608]{0:T(1024)(128)(4,1)}), s8[4194304]{0:T(1024)(128)(4,1)S(1)}, s32[]{:S(2)}) async-start(s8[8388608]{0:T(1024)(128)(4,1)} %bitcast.159), calls=%async_computation | async-start | bytes 8388608
  110.2 12.3 %collective-permute-start.17 = (bf16[1024,128]{1,0:T(8,128)(2,1)S(1)}, bf16[1024,128]{1,0:T(8,128)(2,1)S(1)}, u32[]{:S(2)}, u32[]{:S(2)}) collective-permute-start(bf16[1024,128]{1,0:T(8,128)(2,1)S(1)} %get-tuple-element.443), channel_id=1, source_target_pairs={{4,0},{8,4},{12,8},{5,1},{9,5},{13,9},{6,2},{10,6},{14,10},{7,3},{... | collective-permute-start | bytes 786440 | tf_op jit(solution)/shard_map/ppermute | solution.py:114
  112.1 10.4 %collective-permute-start.18 = (bf16[1024,128]{1,0:T(8,128)(2,1)S(1)}, bf16[1024,128]{1,0:T(8,128)(2,1)S(1)}, u32[]{:S(2)}, u32[]{:S(2)}) collective-permute-start(bf16[1024,128]{1,0:T(8,128)(2,1)S(1)} %get-tuple-element.442), channel_id=1, source_target_pairs={{0,4},{4,8},{8,12},{1,5},{5,9},{9,13},{2,6},{6,10},{10,14},{3,7},{... | collective-permute-start | bytes 786440 | tf_op jit(solution)/shard_map/ppermute | solution.py:113
  117.2 12.1 %collective-permute-start.19 = (bf16[1024,128]{1,0:T(8,128)(2,1)S(1)}, bf16[1024,128]{1,0:T(8,128)(2,1)S(1)}, u32[]{:S(2)}, u32[]{:S(2)}) collective-permute-start(bf16[1024,128]{1,0:T(8,128)(2,1)S(1)} %get-tuple-element.438), channel_id=1, source_target_pairs={{4,0},{8,4},{12,8},{5,1},{9,5},{13,9},{6,2},{10,6},{14,10},{7,3},{... | collective-permute-start | bytes 786440 | tf_op jit(solution)/shard_map/ppermute | solution.py:114
  119.1 10.2 %collective-permute-start.20 = (bf16[1024,128]{1,0:T(8,128)(2,1)S(1)}, bf16[1024,128]{1,0:T(8,128)(2,1)S(1)}, u32[]{:S(2)}, u32[]{:S(2)}) collective-permute-start(bf16[1024,128]{1,0:T(8,128)(2,1)S(1)} %get-tuple-element.437), channel_id=1, source_target_pairs={{0,4},{4,8},{8,12},{1,5},{5,9},{9,13},{2,6},{6,10},{10,14},{3,7},{... | collective-permute-start | bytes 786440 | tf_op jit(solution)/shard_map/ppermute | solution.py:113
  124.0 12.3 %collective-permute-start.21 = (bf16[1024,128]{1,0:T(8,128)(2,1)S(1)}, bf16[1024,128]{1,0:T(8,128)(2,1)S(1)}, u32[]{:S(2)}, u32[]{:S(2)}) collective-permute-start(bf16[1024,128]{1,0:T(8,128)(2,1)S(1)} %get-tuple-element.435), channel_id=1, source_target_pairs={{4,0},{8,4},{12,8},{5,1},{9,5},{13,9},{6,2},{10,6},{14,10},{7,3},{... | collective-permute-start | bytes 786440 | tf_op jit(solution)/shard_map/ppermute | solution.py:114
  126.0 10.4 %collective-permute-start.22 = (bf16[1024,128]{1,0:T(8,128)(2,1)S(1)}, bf16[1024,128]{1,0:T(8,128)(2,1)S(1)}, u32[]{:S(2)}, u32[]{:S(2)}) collective-permute-start(bf16[1024,128]{1,0:T(8,128)(2,1)S(1)} %get-tuple-element.434), channel_id=1, source_target_pairs={{0,4},{4,8},{8,12},{1,5},{5,9},{9,13},{2,6},{6,10},{10,14},{3,7},{... | collective-permute-start | bytes 786440 | tf_op jit(solution)/shard_map/ppermute | solution.py:113
  130.8 11.1 %collective-permute-start.23 = (bf16[1024,128]{1,0:T(8,128)(2,1)S(1)}, bf16[1024,128]{1,0:T(8,128)(2,1)S(1)}, u32[]{:S(2)}, u32[]{:S(2)}) collective-permute-start(bf16[1024,128]{1,0:T(8,128)(2,1)S(1)} %get-tuple-element.432), channel_id=1, source_target_pairs={{4,0},{8,4},{12,8},{5,1},{9,5},{13,9},{6,2},{10,6},{14,10},{7,3},{... | collective-permute-start | bytes 786440 | tf_op jit(solution)/shard_map/ppermute | solution.py:114
  132.8 9.2 %collective-permute-start.24 = (bf16[1024,128]{1,0:T(8,128)(2,1)S(1)}, bf16[1024,128]{1,0:T(8,128)(2,1)S(1)}, u32[]{:S(2)}, u32[]{:S(2)}) collective-permute-start(bf16[1024,128]{1,0:T(8,128)(2,1)S(1)} %get-tuple-element.431), channel_id=1, source_target_pairs={{0,4},{4,8},{8,12},{1,5},{5,9},{9,13},{2,6},{6,10},{10,14},{3,7},{... | collective-permute-start | bytes 786440 | tf_op jit(solution)/shard_map/ppermute | solution.py:113
  136.6 18.7 %collective-permute-start.28 = (bf16[1024,128]{1,0:T(8,128)(2,1)S(1)}, bf16[1024,128]{1,0:T(8,128)(2,1)S(1)}, u32[]{:S(2)}, u32[]{:S(2)}) collective-permute-start(bf16[1024,128]{1,0:T(8,128)(2,1)S(1)} %get-tuple-element.429), channel_id=1, source_target_pairs={{4,0},{8,4},{12,8},{5,1},{9,5},{13,9},{6,2},{10,6},{14,10},{7,3},{... | collective-permute-start | bytes 786440 | tf_op jit(solution)/shard_map/ppermute | solution.py:114
  138.6 16.7 %collective-permute-start.29 = (bf16[1024,128]{1,0:T(8,128)(2,1)S(1)}, bf16[1024,128]{1,0:T(8,128)(2,1)S(1)}, u32[]{:S(2)}, u32[]{:S(2)}) collective-permute-start(bf16[1024,128]{1,0:T(8,128)(2,1)S(1)} %get-tuple-element.428), channel_id=1, source_target_pairs={{0,4},{4,8},{8,12},{1,5},{5,9},{9,13},{2,6},{6,10},{10,14},{3,7},{... | collective-permute-start | bytes 786440 | tf_op jit(solution)/shard_map/ppermute | solution.py:113
  142.2 18.7 %collective-permute-start.30 = (bf16[1024,128]{1,0:T(8,128)(2,1)S(1)}, bf16[1024,128]{1,0:T(8,128)(2,1)S(1)}, u32[]{:S(2)}, u32[]{:S(2)}) collective-permute-start(bf16[1024,128]{1,0:T(8,128)(2,1)S(1)} %get-tuple-element.426), channel_id=1, source_target_pairs={{4,0},{8,4},{12,8},{5,1},{9,5},{13,9},{6,2},{10,6},{14,10},{7,3},{... | collective-permute-start | bytes 786440 | tf_op jit(solution)/shard_map/ppermute | solution.py:114
  144.2 16.7 %collective-permute-start.31 = (bf16[1024,128]{1,0:T(8,128)(2,1)S(1)}, bf16[1024,128]{1,0:T(8,128)(2,1)S(1)}, u32[]{:S(2)}, u32[]{:S(2)}) collective-permute-start(bf16[1024,128]{1,0:T(8,128)(2,1)S(1)} %get-tuple-element.425), channel_id=1, source_target_pairs={{0,4},{4,8},{8,12},{1,5},{5,9},{9,13},{2,6},{6,10},{10,14},{3,7},{... | collective-permute-start | bytes 786440 | tf_op jit(solution)/shard_map/ppermute | solution.py:113
  147.5 24.9 %slice-start.2 = ((s8[8388608]{0:T(1024)(128)(4,1)}), s8[4194304]{0:T(1024)(128)(4,1)S(1)}, s32[]{:S(2)}) async-start(s8[8388608]{0:T(1024)(128)(4,1)} %bitcast.173), calls=%async_computation.2 | async-start | bytes 8388608
  154.0 60.7 %collective-permute-start.26 = (bf16[1024,128]{0,1:T(8,128)(2,1)S(1)}, bf16[1024,128]{0,1:T(8,128)(2,1)S(1)}, u32[]{:S(2)}, u32[]{:S(2)}) collective-permute-start(bf16[1024,128]{0,1:T(8,128)(2,1)S(1)} %bitcast.175), channel_id=1, source_target_pairs={{0,2},{1,3},{2,0},{3,1},{4,6},{5,7},{6,4},{7,5},{8,10},{9,11},{10,... | collective-permute-start | bytes 786440 | tf_op jit(solution)/shard_map/ppermute | solution.py:207
  155.6 10.9 %collective-permute-start.32 = (bf16[1024,128]{1,0:T(8,128)(2,1)S(1)}, bf16[1024,128]{1,0:T(8,128)(2,1)S(1)}, u32[]{:S(2)}, u32[]{:S(2)}) collective-permute-start(bf16[1024,128]{1,0:T(8,128)(2,1)S(1)} %get-tuple-element.423), channel_id=1, source_target_pairs={{4,0},{8,4},{12,8},{5,1},{9,5},{13,9},{6,2},{10,6},{14,10},{7,3},{... | collective-permute-start | bytes 786440 | tf_op jit(solution)/shard_map/ppermute | solution.py:114
  157.6 8.9 %collective-permute-start.33 = (bf16[1024,128]{1,0:T(8,128)(2,1)S(1)}, bf16[1024,128]{1,0:T(8,128)(2,1)S(1)}, u32[]{:S(2)}, u32[]{:S(2)}) collective-permute-start(bf16[1024,128]{1,0:T(8,128)(2,1)S(1)} %get-tuple-element.422), channel_id=1, source_target_pairs={{0,4},{4,8},{8,12},{1,5},{5,9},{9,13},{2,6},{6,10},{10,14},{3,7},{... | collective-permute-start | bytes 786440 | tf_op jit(solution)/shard_map/ppermute | solution.py:113
  161.2 10.9 %collective-permute-start.34 = (bf16[1024,128]{1,0:T(8,128)(2,1)S(1)}, bf16[1024,128]{1,0:T(8,128)(2,1)S(1)}, u32[]{:S(2)}, u32[]{:S(2)}) collective-permute-start(bf16[1024,128]{1,0:T(8,128)(2,1)S(1)} %get-tuple-element.420), channel_id=1, source_target_pairs={{4,0},{8,4},{12,8},{5,1},{9,5},{13,9},{6,2},{10,6},{14,10},{7,3},{... | collective-permute-start | bytes 786440 | tf_op jit(solution)/shard_map/ppermute | solution.py:114
  163.2 8.9 %collective-permute-start.35 = (bf16[1024,128]{1,0:T(8,128)(2,1)S(1)}, bf16[1024,128]{1,0:T(8,128)(2,1)S(1)}, u32[]{:S(2)}, u32[]{:S(2)}) collective-permute-start(bf16[1024,128]{1,0:T(8,128)(2,1)S(1)} %get-tuple-element.419), channel_id=1, source_target_pairs={{0,4},{4,8},{8,12},{1,5},{5,9},{9,13},{2,6},{6,10},{10,14},{3,7},{... | collective-permute-start | bytes 786440 | tf_op jit(solution)/shard_map/ppermute | solution.py:113
  166.8 13.8 %collective-permute-start.39 = (bf16[1024,128]{1,0:T(8,128)(2,1)S(1)}, bf16[1024,128]{1,0:T(8,128)(2,1)S(1)}, u32[]{:S(2)}, u32[]{:S(2)}) collective-permute-start(bf16[1024,128]{1,0:T(8,128)(2,1)S(1)} %get-tuple-element.417), channel_id=1, source_target_pairs={{4,0},{8,4},{12,8},{5,1},{9,5},{13,9},{6,2},{10,6},{14,10},{7,3},{... | collective-permute-start | bytes 786440 | tf_op jit(solution)/shard_map/ppermute | solution.py:114
  168.8 11.8 %collective-permute-start.40 = (bf16[1024,128]{1,0:T(8,128)(2,1)S(1)}, bf16[1024,128]{1,0:T(8,128)(2,1)S(1)}, u32[]{:S(2)}, u32[]{:S(2)}) collective-permute-start(bf16[1024,128]{1,0:T(8,128)(2,1)S(1)} %get-tuple-element.416), channel_id=1, source_target_pairs={{0,4},{4,8},{8,12},{1,5},{5,9},{9,13},{2,6},{6,10},{10,14},{3,7},{... | collective-permute-start | bytes 786440 | tf_op jit(solution)/shard_map/ppermute | solution.py:113
  175.3 10.9 %collective-permute-start.41 = (bf16[1024,128]{1,0:T(8,128)(2,1)S(1)}, bf16[1024,128]{1,0:T(8,128)(2,1)S(1)}, u32[]{:S(2)}, u32[]{:S(2)}) collective-permute-start(bf16[1024,128]{1,0:T(8,128)(2,1)S(1)} %get-tuple-element.414), channel_id=1, source_target_pairs={{4,0},{8,4},{12,8},{5,1},{9,5},{13,9},{6,2},{10,6},{14,10},{7,3},{... | collective-permute-start | bytes 786440 | tf_op jit(solution)/shard_map/ppermute | solution.py:114
  177.4 9.6 %collective-permute-start.42 = (bf16[1024,128]{1,0:T(8,128)(2,1)S(1)}, bf16[1024,128]{1,0:T(8,128)(2,1)S(1)}, u32[]{:S(2)}, u32[]{:S(2)}) collective-permute-start(bf16[1024,128]{1,0:T(8,128)(2,1)S(1)} %get-tuple-element.413), channel_id=1, source_target_pairs={{0,4},{4,8},{8,12},{1,5},{5,9},{9,13},{2,6},{6,10},{10,14},{3,7},{... | collective-permute-start | bytes 786440 | tf_op jit(solution)/shard_map/ppermute | solution.py:113
  180.9 11.6 %collective-permute-start.43 = (bf16[1024,128]{1,0:T(8,128)(2,1)S(1)}, bf16[1024,128]{1,0:T(8,128)(2,1)S(1)}, u32[]{:S(2)}, u32[]{:S(2)}) collective-permute-start(bf16[1024,128]{1,0:T(8,128)(2,1)S(1)} %get-tuple-element.411), channel_id=1, source_target_pairs={{4,0},{8,4},{12,8},{5,1},{9,5},{13,9},{6,2},{10,6},{14,10},{7,3},{... | collective-permute-start | bytes 786440 | tf_op jit(solution)/shard_map/ppermute | solution.py:114
  183.0 9.6 %collective-permute-start.44 = (bf16[1024,128]{1,0:T(8,128)(2,1)S(1)}, bf16[1024,128]{1,0:T(8,128)(2,1)S(1)}, u32[]{:S(2)}, u32[]{:S(2)}) collective-permute-start(bf16[1024,128]{1,0:T(8,128)(2,1)S(1)} %get-tuple-element.410), channel_id=1, source_target_pairs={{0,4},{4,8},{8,12},{1,5},{5,9},{9,13},{2,6},{6,10},{10,14},{3,7},{... | collective-permute-start | bytes 786440 | tf_op jit(solution)/shard_map/ppermute | solution.py:113
  187.2 10.9 %collective-permute-start.45 = (bf16[1024,128]{1,0:T(8,128)(2,1)S(1)}, bf16[1024,128]{1,0:T(8,128)(2,1)S(1)}, u32[]{:S(2)}, u32[]{:S(2)}) collective-permute-start(bf16[1024,128]{1,0:T(8,128)(2,1)S(1)} %get-tuple-element.408), channel_id=1, source_target_pairs={{4,0},{8,4},{12,8},{5,1},{9,5},{13,9},{6,2},{10,6},{14,10},{7,3},{... | collective-permute-start | bytes 786440 | tf_op jit(solution)/shard_map/ppermute | solution.py:114
  189.1 9.0 %collective-permute-start.46 = (bf16[1024,128]{1,0:T(8,128)(2,1)S(1)}, bf16[1024,128]{1,0:T(8,128)(2,1)S(1)}, u32[]{:S(2)}, u32[]{:S(2)}) collective-permute-start(bf16[1024,128]{1,0:T(8,128)(2,1)S(1)} %get-tuple-element.407), channel_id=1, source_target_pairs={{0,4},{4,8},{8,12},{1,5},{5,9},{9,13},{2,6},{6,10},{10,14},{3,7},{... | collective-permute-start | bytes 786440 | tf_op jit(solution)/shard_map/ppermute | solution.py:113
  192.8 13.8 %collective-permute-start.50 = (bf16[1024,128]{1,0:T(8,128)(2,1)S(1)}, bf16[1024,128]{1,0:T(8,128)(2,1)S(1)}, u32[]{:S(2)}, u32[]{:S(2)}) collective-permute-start(bf16[1024,128]{1,0:T(8,128)(2,1)S(1)} %get-tuple-element.405), channel_id=1, source_target_pairs={{4,0},{8,4},{5,1},{9,5},{6,2},{10,6},{7,3},{11,7},{20,16},{24,20},... | collective-permute-start | bytes 786440 | tf_op jit(solution)/shard_map/ppermute | solution.py:114
  194.8 11.9 %collective-permute-start.51 = (bf16[1024,128]{1,0:T(8,128)(2,1)S(1)}, bf16[1024,128]{1,0:T(8,128)(2,1)S(1)}, u32[]{:S(2)}, u32[]{:S(2)}) collective-permute-start(bf16[1024,128]{1,0:T(8,128)(2,1)S(1)} %get-tuple-element.404), channel_id=1, source_target_pairs={{4,8},{8,12},{5,9},{9,13},{6,10},{10,14},{7,11},{11,15},{20,24},{2... | collective-permute-start | bytes 786440 | tf_op jit(solution)/shard_map/ppermute | solution.py:113
  201.3 7.8 %collective-permute-start.52 = (bf16[1024,128]{1,0:T(8,128)(2,1)S(1)}, bf16[1024,128]{1,0:T(8,128)(2,1)S(1)}, u32[]{:S(2)}, u32[]{:S(2)}) collective-permute-start(bf16[1024,128]{1,0:T(8,128)(2,1)S(1)} %get-tuple-element.402), channel_id=1, source_target_pairs={{4,0},{8,4},{5,1},{9,5},{6,2},{10,6},{7,3},{11,7},{20,16},{24,20},... | collective-permute-start | bytes 786440 | tf_op jit(solution)/shard_map/ppermute | solution.py:114
  203.3 6.7 %collective-permute-start.53 = (bf16[1024,128]{1,0:T(8,128)(2,1)S(1)}, bf16[1024,128]{1,0:T(8,128)(2,1)S(1)}, u32[]{:S(2)}, u32[]{:S(2)}) collective-permute-start(bf16[1024,128]{1,0:T(8,128)(2,1)S(1)} %get-tuple-element.401), channel_id=1, source_target_pairs={{4,8},{8,12},{5,9},{9,13},{6,10},{10,14},{7,11},{11,15},{20,24},{2... | collective-permute-start | bytes 786440 | tf_op jit(solution)/shard_map/ppermute | solution.py:113
  207.0 21.2 %collective-permute-start.54 = (bf16[1024,128]{1,0:T(8,128)(2,1)S(1)}, bf16[1024,128]{1,0:T(8,128)(2,1)S(1)}, u32[]{:S(2)}, u32[]{:S(2)}) collective-permute-start(bf16[1024,128]{1,0:T(8,128)(2,1)S(1)} %get-tuple-element.399), channel_id=1, source_target_pairs={{4,0},{5,1},{6,2},{7,3},{20,16},{21,17},{22,18},{23,19}} | collective-permute-start | bytes 786440 | tf_op jit(solution)/shard_map/ppermute | solution.py:114
  208.3 20.0 %collective-permute-start.55 = (bf16[1024,128]{1,0:T(8,128)(2,1)S(1)}, bf16[1024,128]{1,0:T(8,128)(2,1)S(1)}, u32[]{:S(2)}, u32[]{:S(2)}) collective-permute-start(bf16[1024,128]{1,0:T(8,128)(2,1)S(1)} %get-tuple-element.398), channel_id=1, source_target_pairs={{8,12},{9,13},{10,14},{11,15},{24,28},{25,29},{26,30},{27,31}} | collective-permute-start | bytes 786440 | tf_op jit(solution)/shard_map/ppermute | solution.py:113
  212.4 18.2 %collective-permute-start.56 = (bf16[1024,128]{1,0:T(8,128)(2,1)S(1)}, bf16[1024,128]{1,0:T(8,128)(2,1)S(1)}, u32[]{:S(2)}, u32[]{:S(2)}) collective-permute-start(bf16[1024,128]{1,0:T(8,128)(2,1)S(1)} %get-tuple-element.396), channel_id=1, source_target_pairs={{4,0},{5,1},{6,2},{7,3},{20,16},{21,17},{22,18},{23,19}} | collective-permute-start | bytes 786440 | tf_op jit(solution)/shard_map/ppermute | solution.py:114
  213.8 17.5 %collective-permute-start.57 = (bf16[1024,128]{1,0:T(8,128)(2,1)S(1)}, bf16[1024,128]{1,0:T(8,128)(2,1)S(1)}, u32[]{:S(2)}, u32[]{:S(2)}) collective-permute-start(bf16[1024,128]{1,0:T(8,128)(2,1)S(1)} %get-tuple-element.395), channel_id=1, source_target_pairs={{8,12},{9,13},{10,14},{11,15},{24,28},{25,29},{26,30},{27,31}} | collective-permute-start | bytes 786440 | tf_op jit(solution)/shard_map/ppermute | solution.py:113
  214.7 26.6 %collective-permute-start.25 = (bf16[1024,128]{0,1:T(8,128)(2,1)S(1)}, bf16[1024,128]{0,1:T(8,128)(2,1)S(1)}, u32[]{:S(2)}, u32[]{:S(2)}) collective-permute-start(bf16[1024,128]{0,1:T(8,128)(2,1)S(1)} %bitcast.176), channel_id=1, source_target_pairs={{0,1},{1,0},{2,3},{3,2},{4,5},{5,4},{6,7},{7,6},{8,9},{9,8},{10,11... | collective-permute-start | bytes 786440 | tf_op jit(solution)/shard_map/ppermute | solution.py:206
  228.2 14.0 %collective-permute-start.27 = (bf16[1024,128]{0,1:T(8,128)(2,1)S(1)}, bf16[1024,128]{0,1:T(8,128)(2,1)S(1)}, u32[]{:S(2)}, u32[]{:S(2)}) collective-permute-start(bf16[1024,128]{0,1:T(8,128)(2,1)S(1)} %collective-permute-done.26), channel_id=1, source_target_pairs={{0,1},{1,0},{2,3},{3,2},{4,5},{5,4},{6,7},{7,6},{8,9},{9,8},{10,11... | collective-permute-start | bytes 786440 | tf_op jit(solution)/shard_map/ppermute | solution.py:208
  228.3 13.3 %collective-permute-start.37 = (bf16[1024,128]{0,1:T(8,128)(2,1)S(1)}, bf16[1024,128]{0,1:T(8,128)(2,1)}, u32[]{:S(2)}, u32[]{:S(2)}) collective-permute-start(bf16[1024,128]{0,1:T(8,128)(2,1)S(1)} %bitcast.179), channel_id=1, source_target_pairs={{0,2},{1,3},{2,0},{3,1},{4,6},{5,7},{6,4},{7,5},{8,10},{9,11},{10,... | collective-permute-start | bytes 786440 | tf_op jit(solution)/shard_map/ppermute | solution.py:207
  230.6 12.1 %collective-permute-start.36 = (bf16[1024,128]{0,1:T(8,128)(2,1)S(1)}, bf16[1024,128]{0,1:T(8,128)(2,1)S(1)}, u32[]{:S(2)}, u32[]{:S(2)}) collective-permute-start(bf16[1024,128]{0,1:T(8,128)(2,1)S(1)} %bitcast.180), channel_id=1, source_target_pairs={{0,1},{1,0},{2,3},{3,2},{4,5},{5,4},{6,7},{7,6},{8,9},{9,8},{10,11... | collective-permute-start | bytes 786440 | tf_op jit(solution)/shard_map/ppermute | solution.py:206
  231.3 11.0 %collective-permute-start.48 = (bf16[1024,128]{0,1:T(8,128)(2,1)S(1)}, bf16[1024,128]{0,1:T(8,128)(2,1)S(1)}, u32[]{:S(2)}, u32[]{:S(2)}) collective-permute-start(bf16[1024,128]{0,1:T(8,128)(2,1)S(1)} %bitcast.183), channel_id=1, source_target_pairs={{0,2},{1,3},{2,0},{3,1},{4,6},{5,7},{6,4},{7,5},{8,10},{9,11},{10,... | collective-permute-start | bytes 786440 | tf_op jit(solution)/shard_map/ppermute | solution.py:207
  241.3 7.6 %collective-permute-start.59 = (bf16[1024,128]{0,1:T(8,128)(2,1)S(1)}, bf16[1024,128]{0,1:T(8,128)(2,1)S(1)}, u32[]{:S(2)}, u32[]{:S(2)}) collective-permute-start(bf16[1024,128]{0,1:T(8,128)(2,1)S(1)} %bitcast.187), channel_id=1, source_target_pairs={{0,2},{1,3},{2,0},{3,1},{4,6},{5,7},{6,4},{7,5},{8,10},{9,11},{10,... | collective-permute-start | bytes 786440 | tf_op jit(solution)/shard_map/ppermute | solution.py:207
  241.6 8.5 %collective-permute-start.38 = (bf16[1024,128]{0,1:T(8,128)(2,1)}, bf16[1024,128]{0,1:T(8,128)(2,1)S(1)}, u32[]{:S(2)}, u32[]{:S(2)}) collective-permute-start(bf16[1024,128]{0,1:T(8,128)(2,1)} %collective-permute-done.37), channel_id=1, source_target_pairs={{0,1},{1,0},{2,3},{3,2},{4,5},{5,4},{6,7},{7,6},{8,9},{9,8},{10,11... | collective-permute-start | bytes 786440 | tf_op jit(solution)/shard_map/ppermute | solution.py:208
  242.2 7.9 %collective-permute-start.47 = (bf16[1024,128]{0,1:T(8,128)(2,1)S(1)}, bf16[1024,128]{0,1:T(8,128)(2,1)S(1)}, u32[]{:S(2)}, u32[]{:S(2)}) collective-permute-start(bf16[1024,128]{0,1:T(8,128)(2,1)S(1)} %bitcast.184), channel_id=1, source_target_pairs={{0,1},{1,0},{2,3},{3,2},{4,5},{5,4},{6,7},{7,6},{8,9},{9,8},{10,11... | collective-permute-start | bytes 786440 | tf_op jit(solution)/shard_map/ppermute | solution.py:206
  242.3 7.8 %collective-permute-start.49 = (bf16[1024,128]{0,1:T(8,128)(2,1)S(1)}, bf16[1024,128]{0,1:T(8,128)(2,1)S(1)}, u32[]{:S(2)}, u32[]{:S(2)}) collective-permute-start(bf16[1024,128]{0,1:T(8,128)(2,1)S(1)} %collective-permute-done.48), channel_id=1, source_target_pairs={{0,1},{1,0},{2,3},{3,2},{4,5},{5,4},{6,7},{7,6},{8,9},{9,8},{10,11... | collective-permute-start | bytes 786440 | tf_op jit(solution)/shard_map/ppermute | solution.py:208
  242.7 7.4 %collective-permute-start.58 = (bf16[1024,128]{0,1:T(8,128)(2,1)S(1)}, bf16[1024,128]{0,1:T(8,128)(2,1)S(1)}, u32[]{:S(2)}, u32[]{:S(2)}) collective-permute-start(bf16[1024,128]{0,1:T(8,128)(2,1)S(1)} %bitcast.188), channel_id=1, source_target_pairs={{0,1},{1,0},{2,3},{3,2},{4,5},{5,4},{6,7},{7,6},{8,9},{9,8},{10,11... | collective-permute-start | bytes 786440 | tf_op jit(solution)/shard_map/ppermute | solution.py:206
  248.9 2.5 collective-permute-start.60
  257.2 37.5 %collective-permute-start.61 = (bf16[512,512]{1,0:T(8,128)(2,1)S(1)}, bf16[512,512]{1,0:T(8,128)(2,1)S(1)}, u32[]{:S(2)}, u32[]{:S(2)}) collective-permute-start(bf16[512,512]{1,0:T(8,128)(2,1)S(1)} %get-tuple-element.464), channel_id=1, source_target_pairs={{0,4},{4,8},{8,12},{12,0},{1,5},{5,9},{9,13},{13,1},{2,6},{6,10},{... | collective-permute-start | bytes 1572872 | tf_op jit(solution)/shard_map/ppermute | solution.py:224
  261.2 44.6 %collective-permute-start.62 = (bf16[512,512]{1,0:T(8,128)(2,1)S(1)}, bf16[512,512]{1,0:T(8,128)(2,1)S(1)}, u32[]{:S(2)}, u32[]{:S(2)}) collective-permute-start(bf16[512,512]{1,0:T(8,128)(2,1)S(1)} %get-tuple-element.466), channel_id=1, source_target_pairs={{0,8},{4,12},{8,0},{12,4},{1,9},{5,13},{9,1},{13,5},{2,10},{6,14},... | collective-permute-start | bytes 1572872 | tf_op jit(solution)/shard_map/ppermute | solution.py:224
  261.2 45.6 %collective-permute-start.63 = (bf16[512,512]{1,0:T(8,128)(2,1)S(1)}, bf16[512,512]{1,0:T(8,128)(2,1)S(1)}, u32[]{:S(2)}, u32[]{:S(2)}) collective-permute-start(bf16[512,512]{1,0:T(8,128)(2,1)S(1)} %get-tuple-element.465), channel_id=1, source_target_pairs={{0,12},{4,0},{8,4},{12,8},{1,13},{5,1},{9,5},{13,9},{2,14},{6,2},{... | collective-permute-start | bytes 1572872 | tf_op jit(solution)/shard_map/ppermute | solution.py:224
  (7 other events, 70.1 us)

commit v2 on v0

v2 whole, which is shorter than its diff:
```python
import functools

import jax
import jax.numpy as jnp
from jax import lax
from jax.experimental import pallas as pl
from jax.experimental.pallas import tpu as pltpu
from jax.sharding import PartitionSpec as P

LANES = 128
CHUNKS = 16
LAG = 2
UNROLL = 2


def rotation(size, by):
    return [(i, (i + by) % size) for i in range(size)]


def flipped(size, bit):
    return [(i, i ^ bit) for i in range(size)]


def over_members(array, axis, size):
    held = {0: array}
    bit = size // 2
    while bit:
        held |= {e | bit: lax.ppermute(a, axis, flipped(size, bit)) for e, a in held.items()}
        bit //= 2
    return [held[e] for e in range(size)]


def spread_kernel(planes, across, cap, place, table_aux, table_basis, begins, counts, own_tiles, *refs):
    received = refs[:-8]
    overflow, panels, sums, held, chosen, owners, bases, arrived = refs[-8:]
    slots, tile = own_tiles.shape[:2]
    part = cap // across
    batch = part * (planes - 1)
    position, member, rounds = place[0], place[1], place[2]
    local_bases = panels.shape[0] // tile
    groups = sums.shape[0]

    copies, at = [], 0
    for n, tiles in enumerate(received):
        copies.append(pltpu.make_async_copy(tiles, held.at[pl.ds(at, tiles.shape[0])], arrived.at[n]))
        at += tiles.shape[0]
    for copy in copies:
        copy.start()
    sums[...] = jnp.zeros_like(sums)

    def rows_of(source, slot):
        return table_aux[source, slot] * tile, (table_basis[source, slot] - position * local_bases) * tile

    def ranges(turn, side, source):
        first = begins[source, position] + turn * cap
        last = jnp.minimum(first + cap, begins[source, position] + counts[source, position])
        begin = jnp.minimum(first, slots - cap) + side * part
        return begin, jnp.clip(first - begin, 0, part), jnp.clip(last - begin, 0, part)

    def term_of(block, base):
        panel = panels[pl.ds(pl.multiple_of(base, tile), tile), :]
        return jnp.dot(block, panel, preferred_element_type=jnp.float32)

    def add(owner, term):
        for g in range(groups):
            sums[g, pl.ds(pl.multiple_of(owner, tile), tile), :] += term[:, g * LANES : (g + 1) * LANES]

    count = jnp.int32(0)
    for e in range(across):
        for q in range(planes - 1):
            source = lax.rem(position + (planes - 1 - q), planes)
            begin, low, high = ranges(0, member ^ e, source)

            def note(i, count, e=e, q=q, source=source, begin=begin):
                chosen[count] = e * batch + q * part + i
                owners[count], bases[count] = rows_of(source, begin + i)
                return count + 1

            count = lax.fori_loop(low, high, note, count)
    for i in range(UNROLL - 1):
        chosen[count + i] = 0
        owners[count + i] = 0
        bases[count + i] = 0

    own_first = begins[position, position]
    own_count = counts[position, position]

    def several_own(n, _):
        terms = []
        for i in range(UNROLL):
            used = n * UNROLL + i < own_count
            slot = jnp.minimum(own_first + n * UNROLL + i, slots - 1)
            owner, base = rows_of(position, slot)
            term = term_of(own_tiles[slot], jnp.where(used, base, 0))
            terms.append((owner, jnp.where(used, term, 0.0)))
        for owner, term in terms:
            add(owner, term)
        return 0

    lax.fori_loop(0, (own_count + UNROLL - 1) // UNROLL, several_own, 0)
    for copy in copies:
        copy.wait()

    def several(n, _):
        terms = []
        for i in range(UNROLL):
            at = n * UNROLL + i
            term = term_of(held[chosen[at]], bases[at])
            terms.append((owners[at], jnp.where(at < count, term, 0.0)))
        for owner, term in terms:
            add(owner, term)
        return 0

    lax.fori_loop(0, (count + UNROLL - 1) // UNROLL, several, 0)

    def late_round(turn, _):
        def late_part(n, _):
            e, q = n // (planes - 1), lax.rem(n, planes - 1)
            source = lax.rem(position + (planes - 1 - q), planes)
            begin, low, high = ranges(turn, member ^ e, source)

            def late_one(i, _):
                pltpu.sync_copy(overflow.at[turn - 1, e, q * part + i], held.at[0])
                owner, base = rows_of(source, begin + i)
                add(owner, term_of(held[0], base))
                return 0

            return lax.fori_loop(low, high, late_one, 0)

        return lax.fori_loop(0, across * (planes - 1), late_part, 0)

    lax.fori_loop(1, rounds, late_round, 0)


def spread(place, tables, tiles, received, overflow, orbitals, rows, planes, across, cap):
    slots, tile = tiles.shape[:2]
    most = sum(r.shape[0] for r in received)
    smem = pl.BlockSpec(memory_space=pltpu.SMEM)
    vmem = pl.BlockSpec(memory_space=pltpu.VMEM)
    hbm = pl.BlockSpec(memory_space=pltpu.HBM)
    return pl.pallas_call(
        functools.partial(spread_kernel, planes, across, cap),
        out_shape=jax.ShapeDtypeStruct((orbitals.shape[1] // LANES, rows, LANES), jnp.float32),
        in_specs=[smem] * 5 + [vmem] * (1 + len(received)) + [hbm, vmem],
        out_specs=vmem,
        scratch_shapes=[
            pltpu.VMEM((most, tile, tile), tiles.dtype),
            pltpu.SMEM((most + UNROLL,), jnp.int32),
            pltpu.SMEM((most + UNROLL,), jnp.int32),
            pltpu.SMEM((most + UNROLL,), jnp.int32),
            pltpu.SemaphoreType.DMA((len(received),)),
        ],
        compiler_params=pltpu.CompilerParams(vmem_limit_bytes=24 * 1024 * 1024),
        cost_estimate=pl.CostEstimate(
            flops=2 * slots * tile * tile * orbitals.shape[1],
            bytes_accessed=24 * 1024 * 1024,
            transcendentals=0,
        ),
    )(place, *tables, tiles, *received, overflow, orbitals)


def stage_kernel(steps, tiles, source, staged, largest, arrived):
    size = source.shape[0] // steps

    def piece(n):
        rows = pl.ds(n * size, size)
        return pltpu.make_async_copy(source.at[rows], staged.at[rows], arrived.at[n])

    for n in range(steps):
        piece(n).start()
    lanes = tiles.shape[-1]
    best = jnp.max(jnp.abs(tiles[...].reshape(-1, 16, lanes)), axis=0)
    largest[0] = best.astype(jnp.float32)
    most = None
    for n in range(steps):
        piece(n).wait()
        block = jnp.abs(staged[pl.ds(n * size, size), :]).reshape(-1, 16, source.shape[1])
        found = jnp.max(block, axis=0)
        most = found if most is None else jnp.maximum(most, found)
    across = most[:, :lanes]
    for g in range(1, source.shape[1] // lanes):
        across = jnp.maximum(across, most[:, g * lanes : (g + 1) * lanes])
    largest[1] = across.astype(jnp.float32)


def stage(tiles, orbitals):
    steps = 8
    vmem = pl.BlockSpec(memory_space=pltpu.VMEM)
    return pl.pallas_call(
        functools.partial(stage_kernel, steps),
        out_shape=(
            jax.ShapeDtypeStruct(orbitals.shape, orbitals.dtype),
            jax.ShapeDtypeStruct((2, 16, tiles.shape[-1]), jnp.float32),
        ),
        in_specs=[vmem, pl.BlockSpec(memory_space=pltpu.HBM)],
        out_specs=(vmem, vmem),
        scratch_shapes=[pltpu.SemaphoreType.DMA((steps,))],
        compiler_params=pltpu.CompilerParams(vmem_limit_bytes=16 * 1024 * 1024),
        cost_estimate=pl.CostEstimate(flops=0, bytes_accessed=10 * 1024 * 1024, transcendentals=0),
    )(tiles, orbitals)


def unfilled(shape, dtype):
    return pl.pallas_call(
        lambda out: None,
        out_shape=jax.ShapeDtypeStruct(shape, dtype),
        out_specs=pl.BlockSpec(memory_space=pltpu.HBM),
    )()


def all_planes(partial, consume, at_step, groups, rows, planes, position, scale):
    half = planes // 2
    per_group = CHUNKS // groups
    size = rows // per_group
    hops = planes - 1
    mirrored = hops - position
    in_left = position < half
    far = jnp.maximum(position, mirrored)
    got_right, got_left, paid_right, paid_left, done = {}, {}, {}, {}, {}
    total_steps = CHUNKS + LAG * hops

    def own_rows(s, rank):
        chunks = [s - LAG * r for r in range(half)]
        if not any(0 <= c < CHUNKS for c in chunks):
            return None
        at = jnp.clip(s - LAG * rank, 0, CHUNKS - 1) * size
        return lax.dynamic_slice_in_dim(partial, at, size, 0)

    def payload(s, rank, got, paid_other):
        rows = own_rows(s, rank)
        total = None if rows is None else rows * scale
        before = got.get(s - LAG)
        if before is not None:
            crossing = jnp.where(rank == half, paid_other[s - LAG].astype(jnp.float32), 0.0)
            added = crossing if total is None else jnp.where(rank < half, total, crossing)
            total = before.astype(jnp.float32) + added
        return total.astype(jnp.float16)

    def finished(group):
        pieces = []
        for k in range(group * per_group, (group + 1) * per_group):
            chunk = None
            for r in range(half, planes):
                this = done[k + LAG * r]
                chunk = this if chunk is None else jnp.where(far == r, this, chunk)
            pieces.append(chunk)
        whole = jnp.concatenate(pieces, axis=0).astype(jnp.float32)
        return lax.optimization_barrier((whole * (1.0 / scale)).astype(jnp.bfloat16))

    waiting = []
    for s in range(total_steps):
        if s - LAG in got_right:
            got_right[s - LAG], got_left[s - LAG], *_ = lax.optimization_barrier(
                (got_right[s - LAG], got_left[s - LAG], paid_right[s - 1], paid_left[s - 1], *waiting)
            )
            waiting = []
        paid_right[s] = payload(s, position, got_right, paid_left)
        paid_left[s] = payload(s, mirrored, got_left, paid_right)
        right = [(i, i + 1) for i in range(hops) if 0 <= s - LAG * i < CHUNKS]
        if right:
            got_right[s] = lax.ppermute(paid_right[s], "aux", right)
            got_left[s] = lax.ppermute(paid_left[s], "aux", [(hops - i, hops - j) for i, j in right])
        done[s] = jnp.where(in_left, paid_left[s], paid_right[s])
        group, rest = divmod(s - LAG * hops + 1, per_group)
        if group > 0 and rest == 0:
            waiting.append(consume(group - 1, finished(group - 1)))
        waiting += at_step(total_steps - s)


def shards(tiles, slot_aux, slot_basis, slot_count, orbitals, fit_rows, *, groups, planes, across):
    position = lax.axis_index("aux")
    member = lax.axis_index("orb")
    slots, tile = tiles.shape[:2]
    aux_rows = fit_rows.shape[1]
    width = orbitals.shape[1]
    local_bases = orbitals.shape[0] // tile
    cap = min(slots, across * -(-7 * slots // (4 * planes * across)))
    part = cap // across
    later = -(-slots // cap) - 1

    live = jnp.arange(slots, dtype=jnp.int32)[None, :] < slot_count[:, None]
    target = jnp.where(live, slot_basis // local_bases, planes)
    plane_ids = jnp.arange(planes, dtype=jnp.int32)
    begins = jnp.sum(target[:, None, :] < plane_ids[None, :, None], axis=2, dtype=jnp.int32)
    counts = jnp.sum(target[:, None, :] == plane_ids[None, :, None], axis=2, dtype=jnp.int32)
    away = jnp.where(plane_ids[:, None] == plane_ids[None, :], 0, counts)
    rounds = (jnp.max(away) + cap - 1) // cap
    send_first = lax.dynamic_index_in_dim(begins, position, 0, keepdims=False)

    def exchange(turn):
        chosen = []
        for by in range(1, planes):
            first = send_first[(position + by) % planes] + turn * cap
            begin = jnp.minimum(first, slots - cap) + member * part
            chosen.append(lax.dynamic_slice_in_dim(tiles, begin, part, 0))
        chosen = lax.optimization_barrier(chosen)
        sent = [lax.ppermute(c, "aux", rotation(planes, by)) for by, c in enumerate(chosen, 1)]
        return chosen, sent

    def gather(sent):
        if planes > 4:
            sent = [jnp.concatenate(sent, axis=0)]
        held = [over_members(arrived, "orb", across) for arrived in sent]
        return [[h[e] for h in held] for e in range(across)]

    chosen, sent = exchange(jnp.int32(0))
    all_tiles, all_orbitals, _ = lax.optimization_barrier((tiles, orbitals, chosen))
    panels, largest = stage(all_tiles, all_orbitals)
    largest = jnp.max(largest, axis=(1, 2))
    *sent, largest, rounds = lax.optimization_barrier((*sent, largest, rounds))
    largest = jnp.broadcast_to(largest[:, None], (2, LANES))
    others = [lax.ppermute(largest, "aux", rotation(planes, by)) for by in range(1, planes)]
    most = rounds
    for by in range(1, groups):
        most = jnp.maximum(most, lax.ppermute(rounds, "groups", rotation(groups, by)))
    received = [part_tiles for entry in gather(sent) for part_tiles in entry]
    for other in others:
        largest = jnp.maximum(largest, other)
    bound = tile * jnp.sum(counts).astype(jnp.float32) * largest[0, 0] * largest[1, 0]
    scale = 32768.0 / jnp.maximum(bound, 1e-30)

    def more(state):
        turn, kept = state
        tiles_now = jnp.stack([jnp.concatenate(entry, axis=0) for entry in gather(exchange(turn)[1])])
        return turn + 1, lax.dynamic_update_index_in_dim(kept, tiles_now, turn - 1, 0)

    batch = (planes - 1) * part
    empty = unfilled((max(later, 1), across, batch, tile, tile), tiles.dtype)
    _, overflow = lax.while_loop(lambda state: state[0] < most, more, (jnp.int32(1), empty))
    place = jnp.stack([position, member, most]).astype(jnp.int32)

    tables = (slot_aux, slot_basis, begins, counts)
    partial = spread(place, tables, tiles, received, overflow, panels, aux_rows, planes, across, cap)
    partial = partial.reshape(-1, LANES)
    column_groups = width // LANES
    fitted, wide = [], []
    square = planes == across
    blocks = {}

    def product(left, right):
        return jnp.einsum("pj,pi->ji", left, right, preferred_element_type=jnp.float32)

    def scatter(parts):
        stacked = jnp.stack(parts)

        def to(plane):
            return lax.dynamic_index_in_dim(stacked, plane ^ member, 0, keepdims=False)

        sent = [to((position + by) % planes).astype(jnp.bfloat16) for by in range(1, planes)]
        return [to(position)] + [lax.ppermute(t, "aux", rotation(planes, by)) for by, t in enumerate(sent, 1)]

    def total(terms):
        return sum((t.astype(jnp.float32) for t in terms[1:]), terms[0])

    def consume(g, rounded):
        last = g == column_groups - 1
        if square and last:
            rounded, blocks["corner"][1] = lax.optimization_barrier((rounded, blocks["corner"][1]))
        own = jnp.dot(fit_rows, rounded, preferred_element_type=jnp.float32).astype(jnp.bfloat16)
        if square and last:
            blocks["upper"] = scatter([product(w, own) for w in blocks["early"]])
        fitted.append(own)
        if square:
            wide.append(over_members(own, "orb", across))
        if square and g == column_groups - 2:
            blocks["early"] = [jnp.concatenate([w[e] for w in wide], axis=1) for e in range(across)]
            inner = jnp.concatenate(fitted, axis=1)
            blocks["terms"] = [product(w, inner) for w in blocks["early"]]
        return own

    def at_step(steps_left):
        if "terms" in blocks and "corner" not in blocks and steps_left <= 3:
            blocks["corner"] = scatter(blocks["terms"])
            return list(blocks["terms"])
        return []

    all_planes(partial, consume, at_step, column_groups, aux_rows, planes, position, scale)
    fitted = jnp.concatenate(fitted, axis=1)
    if square:
        lower = total(scatter([product(w, fitted) for w in wide[-1]]))
        upper = jnp.concatenate([total(blocks["corner"]), total(blocks["upper"])], axis=1)
        return jnp.concatenate([upper, lower], axis=0)
    wide = lax.all_gather(fitted, "orb", axis=1, tiled=True)
    return lax.psum_scatter(product(wide, fitted), "aux", scatter_dimension=0, tiled=True)


def solution(mesh):
    body = functools.partial(
        shards,
        groups=mesh.shape["groups"],
        planes=mesh.shape["aux"],
        across=mesh.shape["orb"],
    )
    return jax.shard_map(
        body,
        mesh=mesh,
        in_specs=(
            P(("groups", "aux"), None, None),
            P("groups", None),
            P("groups", None),
            P("groups"),
            P(("groups", "aux"), "orb"),
            P(("groups", "aux"), None),
        ),
        out_specs=P(("groups", "aux"), "orb"),
        check_vma=False,
    )
```

time: 1160 us -> 272 us (0.23)
  waiting for transfers between devices: 861 us -> 53.7 us
  local copies, waits for them, and re-layouts: 218 us -> 18.8 us
  starting transfers between devices: 0.35 us -> 145 us
  matrix products: 53.3 us -> 17.1 us
  Pallas kernels: 0 us -> 14 us
    all_gather x3 -> x0, waiting for transfers between devices: 638 us -> none  [the longest x1 523 us: shards(): whole_panel = lax.all_gather(orbitals, 'aux', axis=0, tiled=True)]
    reduce_scatter x2 -> x0, waiting for transfers between devices: 222 us -> none  [the longest x1 145 us: shards(): lax.psum_scatter(running, 'aux', scatter_dimension=0, tiled=True)]
    gather x192 -> x0, local copies, waits for them, and re-layouts: 180 us -> none
    ppermute x0 -> x77, starting transfers between devices: none -> 145 us  [the longest x20 54.5 us: all_planes(): got_right[s] = lax.ppermute(paid_right[s], 'aux', right)]
    ppermute x0 -> x77, waiting for transfers between devices: none -> 53.7 us  [the longest x9 22.5 us: scatter(): lax.ppermute(t, 'aux', rotation(planes, by))]
    dot_general x6 -> x16, matrix products: 53.3 us -> 17.1 us  [the longest x4 11.5 us: consume(): jnp.dot(fit_rows, rounded, preferred_element_type=jnp.float32)]
    pad x1 -> x0, local copies, waits for them, and re-layouts: 21.3 us -> none  [run_slots(): padded = jnp.pad(panel_piece, ((tile_width, tile_width), (0, 0)))]
    unnamed x8 -> x26, local copies, waits for them, and re-layouts: 0.02 us -> 14.7 us
  transfers between devices with their start and end apart: 5 -> 77, of which waited for: 5 -> 21; matrix products, arithmetic and copies ran while one was open for 0% -> 12% of each run, Pallas kernels for 0% -> 1%
where the time goes in v2:
time: 272 us; the launch traced here: 271 us
  starting transfers between devices  145 us (53%)
  waiting for transfers between devices  53.7 us (20%)
  local copies, waits for them, and re-layouts  18.8 us (7%)
  matrix products  17.1 us (6%)
  other arithmetic  16.5 us (6%)
  Pallas kernels  14 us (5%)
  between operations  6.38 us (2%)
    ppermute x20, starting transfers between devices, all_planes(): got_right[s] = lax.ppermute(paid_right[s], 'aux', right)  54.5 us
    ppermute x20, starting transfers between devices, all_planes(): lax.ppermute(paid_left[s], 'aux', [(hops - i, hops - j) for i, j in right])  38.1 us
    ppermute x21, starting transfers between devices, over_members(): lax.ppermute(a, axis, flipped(size, bit))  35.8 us
    ppermute x9, waiting for transfers between devices, scatter(): lax.ppermute(t, 'aux', rotation(planes, by))  22.5 us
    unnamed x26, local copies, waits for them, and re-layouts  14.7 us
    ppermute x20, waiting for transfers between devices, all_planes(): got_right[s] = lax.ppermute(paid_right[s], 'aux', right)  11.7 us
    dot_general x4, matrix products, consume(): jnp.dot(fit_rows, rounded, preferred_element_type=jnp.float32)  11.5 us
    pallas_call x1, Pallas kernels, spread(): pl.pallas_call(functools.partial(spread_kernel, planes, across, cap), out...  10.4 us
  transfers between devices with their start and end apart: 77, of which 21 were waited for; matrix products, arithmetic and copies ran while one was open for 12% of the time, Pallas kernels for 1%

profile of v2, /device:TPU:13, one launch (start us, length us, event | category | flops | bytes accessed | tf_op | source)
XLA Modules:
  0.0 271.4 jit_solution(16941905181171974059)
XLA Ops:
  11.9 3.2 %copy-done.2 = bf16[7680,512]{1,0:T(8,128)(2,1)S(1)} copy-done((bf16[7680,512]{1,0:T(8,128)(2,1)S(1)}, bf16[7680,512]{1,0:T(8,128)(2,1)}, u32[]{:S(2)}) %copy-start.2) | copy-done | bytes 7864344
  15.1 3.6 %shard_map.64 = (bf16[7680,512]{1,0:T(8,128)(2,1)S(1)}, f32[2,16,128]{2,1,0:T(8,128)S(1)}) custom-call(bf16[64,128,128]{2,1,0:T(8,128)(2,1)S(1)} %copy-done.7, bf16[7680,512]{1,0:T(8,128)(2,1)S(1)} %copy-done.2), custom_call_target="tpu_custom_call" | custom-call | bytes 10485760 | tf_op jit(solution)/shard_map/pallas_call | solution.py:189
  18.8 3.2 %copy-done.3 = bf16[7680,512]{1,0:T(8,128)(2,1)} copy-done((bf16[7680,512]{1,0:T(8,128)(2,1)}, bf16[7680,512]{1,0:T(8,128)(2,1)S(1)}, u32[]{:S(2)}) %copy-start.3) | copy-done | bytes 7864344
  22.1 3.5 %collective-permute-done.13.refs_1_ = bf16[7,128,128]{2,1,0:T(8,128)(2,1)S(1)} collective-permute-done((bf16[7,128,128]{2,1,0:T(8,128)(2,1)S(1)}, bf16[7,128,128]{2,1,0:T(8,128)(2,1)S(1)}, u32[]{:S(2)}, u32[]{:S(2)}) %collective-permute-start.13) | collective-permute-done | bytes 229408 | tf_op jit(solution)/shard_map/ppermute | solution.py:297
  25.6 2.8 %collective-permute-done.14.refs_2_ = bf16[7,128,128]{2,1,0:T(8,128)(2,1)S(1)} collective-permute-done((bf16[7,128,128]{2,1,0:T(8,128)(2,1)S(1)}, bf16[7,128,128]{2,1,0:T(8,128)(2,1)S(1)}, u32[]{:S(2)}, u32[]{:S(2)}) %collective-permute-start.14) | collective-permute-done | bytes 229408 | tf_op jit(solution)/shard_map/ppermute | solution.py:297
  34.2 2.6 collective-permute-start.16
  36.9 2.7 collective-permute-done.25
  43.7 1.9 collective-permute-done.27
  45.6 2.9 %collective-permute-start.17 = (bf16[7,128,128]{2,1,0:T(8,128)(2,1)S(1)}, bf16[7,128,128]{2,1,0:T(8,128)(2,1)S(1)}, u32[]{:S(2)}, u32[]{:S(2)}) collective-permute-start(bf16[7,128,128]{2,1,0:T(8,128)(2,1)S(1)} %collective-permute-done.13.refs_1_), channel_id=1, source_target_pairs={{0,1},{1,0},{2,3},{3,2},{4,5},{5,4},{6,7},{7,6},{8,9},{9,8},{10,11... | collective-permute-start | bytes 688136 | tf_op jit(solution)/shard_map/ppermute | solution.py:28
  51.6 3.2 %copy-done.4 = bf16[7680,512]{1,0:T(8,128)(2,1)S(1)} copy-done((bf16[7680,512]{1,0:T(8,128)(2,1)S(1)}, bf16[7680,512]{1,0:T(8,128)(2,1)}, u32[]{:S(2)}) %copy-start.4) | copy-done | bytes 7864344
  54.9 10.4 %shard_map.66 = f32[4,4096,128]{2,1,0:T(8,128)S(1)} custom-call(s32[3]{0:T(128)S(1)} %pad_add_fusion.place, s32[4,64]{1,0:T(4,128)S(1)} %copy-done.6, s32[4,64]{1,0:T(4,128)S(1)} %copy-done.5, s32[4,4]{1,0:T(4,128)S(1)} %get-tuple-element.315.begins, s32[4,4]{1,0:T(4,128)S(1)} %get-tuple-element.314.counts, bf16[64,128,128]{2,1,0:T(8,128)(2,1)} %own_tiles.1, ...), custom_call_target="tpu_custom_call" | custom-call | flops 1073741824 | bytes 25165824 | tf_op jit(solution)/shard_map/pallas_call | solution.py:141
  65.3 3.3 %copy-done = f32[4,4096,128]{2,1,0:T(8,128)} copy-done((f32[4,4096,128]{2,1,0:T(8,128)}, f32[4,4096,128]{2,1,0:T(8,128)S(1)}, u32[]{:S(2)}) %copy-start) | copy-done | bytes 8388632
  72.9 5.4 %collective-permute-done.28 = f16[1024,128]{1,0:T(8,128)(2,1)S(1)} collective-permute-done((f16[1024,128]{1,0:T(8,128)(2,1)S(1)}, f16[1024,128]{1,0:T(8,128)(2,1)S(1)}, u32[]{:S(2)}, u32[]{:S(2)}) %collective-permute-start.28) | collective-permute-done | bytes 262176 | tf_op jit(solution)/shard_map/ppermute | solution.py:261
  79.9 4.7 %collective-permute-start.30 = (f16[1024,128]{1,0:T(8,128)(2,1)S(1)}, f16[1024,128]{1,0:T(8,128)(2,1)S(1)}, u32[]{:S(2)}, u32[]{:S(2)}) collective-permute-start(f16[1024,128]{1,0:T(8,128)(2,1)S(1)} %get-tuple-element.387), channel_id=1, source_target_pairs={{0,4},{4,8},{1,5},{5,9},{2,6},{6,10},{3,7},{7,11},{16,20},{20,24},... | collective-permute-start | bytes 786440 | tf_op jit(solution)/shard_map/ppermute | solution.py:261
  87.4 4.0 %collective-permute-start.36 = (f16[1024,128]{1,0:T(8,128)(2,1)S(1)}, f16[1024,128]{1,0:T(8,128)(2,1)S(1)}, u32[]{:S(2)}, u32[]{:S(2)}) collective-permute-start(f16[1024,128]{1,0:T(8,128)(2,1)S(1)} %get-tuple-element.385), channel_id=1, source_target_pairs={{0,4},{4,8},{1,5},{5,9},{2,6},{6,10},{3,7},{7,11},{16,20},{20,24},... | collective-permute-start | bytes 786440 | tf_op jit(solution)/shard_map/ppermute | solution.py:261
  94.3 4.0 %collective-permute-start.34 = (f16[1024,128]{1,0:T(8,128)(2,1)S(1)}, f16[1024,128]{1,0:T(8,128)(2,1)S(1)}, u32[]{:S(2)}, u32[]{:S(2)}) collective-permute-start(f16[1024,128]{1,0:T(8,128)(2,1)S(1)} %get-tuple-element.383), channel_id=1, source_target_pairs={{0,4},{4,8},{8,12},{1,5},{5,9},{9,13},{2,6},{6,10},{10,14},{3,7},{... | collective-permute-start | bytes 786440 | tf_op jit(solution)/shard_map/ppermute | solution.py:261
  98.3 1.9 collective-permute-start.35
  101.9 3.4 %collective-permute-start.38 = (f16[1024,128]{1,0:T(8,128)(2,1)S(1)}, f16[1024,128]{1,0:T(8,128)(2,1)S(1)}, u32[]{:S(2)}, u32[]{:S(2)}) collective-permute-start(f16[1024,128]{1,0:T(8,128)(2,1)S(1)} %get-tuple-element.380), channel_id=1, source_target_pairs={{0,4},{4,8},{8,12},{1,5},{5,9},{9,13},{2,6},{6,10},{10,14},{3,7},{... | collective-permute-start | bytes 786440 | tf_op jit(solution)/shard_map/ppermute | solution.py:261
  105.3 1.9 collective-permute-start.39
  107.6 3.4 %collective-permute-start.40 = (f16[1024,128]{1,0:T(8,128)(2,1)S(1)}, f16[1024,128]{1,0:T(8,128)(2,1)S(1)}, u32[]{:S(2)}, u32[]{:S(2)}) collective-permute-start(f16[1024,128]{1,0:T(8,128)(2,1)S(1)} %get-tuple-element.367), channel_id=1, source_target_pairs={{0,4},{4,8},{8,12},{1,5},{5,9},{9,13},{2,6},{6,10},{10,14},{3,7},{... | collective-permute-start | bytes 786440 | tf_op jit(solution)/shard_map/ppermute | solution.py:261
  111.0 2.2 collective-permute-start.41
  113.6 3.3 %collective-permute-start.42 = (f16[1024,128]{1,0:T(8,128)(2,1)S(1)}, f16[1024,128]{1,0:T(8,128)(2,1)S(1)}, u32[]{:S(2)}, u32[]{:S(2)}) collective-permute-start(f16[1024,128]{1,0:T(8,128)(2,1)S(1)} %get-tuple-element.370), channel_id=1, source_target_pairs={{0,4},{4,8},{8,12},{1,5},{5,9},{9,13},{2,6},{6,10},{10,14},{3,7},{... | collective-permute-start | bytes 786440 | tf_op jit(solution)/shard_map/ppermute | solution.py:261
  117.0 2.0 collective-permute-start.43
  119.6 3.0 %collective-permute-start.44 = (f16[1024,128]{1,0:T(8,128)(2,1)S(1)}, f16[1024,128]{1,0:T(8,128)(2,1)S(1)}, u32[]{:S(2)}, u32[]{:S(2)}) collective-permute-start(f16[1024,128]{1,0:T(8,128)(2,1)S(1)} %get-tuple-element.373), channel_id=1, source_target_pairs={{0,4},{4,8},{8,12},{1,5},{5,9},{9,13},{2,6},{6,10},{10,14},{3,7},{... | collective-permute-start | bytes 786440 | tf_op jit(solution)/shard_map/ppermute | solution.py:261
  122.7 2.4 collective-permute-start.45
  126.5 2.9 %fusion.1 = bf16[1024,128]{0,1:T(8,128)(2,1)S(1)} fusion(bf16[4096,128]{1,0:T(8,128)(2,1)S(1)} %multiply_convert_fusion.3, bf16[1024,4096]{1,0:T(8,128)(2,1)S(1)} %bitcast.146), kind=kOutput, calls=%fused_computation.22 | convolution fusion | flops 1073872896 | bytes 9699328 | tf_op jit(solution)/shard_map/dot_general | solution.py:359
  130.4 6.8 %collective-permute-start.60 = (bf16[1024,128]{0,1:T(8,128)(2,1)S(1)}, bf16[1024,128]{0,1:T(8,128)(2,1)S(1)}, u32[]{:S(2)}, u32[]{:S(2)}) collective-permute-start(bf16[1024,128]{0,1:T(8,128)(2,1)S(1)} %fusion.1), channel_id=1, source_target_pairs={{0,1},{1,0},{2,3},{3,2},{4,5},{5,4},{6,7},{7,6},{8,9},{9,8},{10,11... | collective-permute-start | bytes 786440 | tf_op jit(solution)/shard_map/ppermute | solution.py:28
  137.3 1.9 collective-permute-start.46
  139.2 3.4 %collective-permute-start.47 = (f16[1024,128]{1,0:T(8,128)(2,1)S(1)}, f16[1024,128]{1,0:T(8,128)(2,1)S(1)}, u32[]{:S(2)}, u32[]{:S(2)}) collective-permute-start(f16[1024,128]{1,0:T(8,128)(2,1)S(1)} %get-tuple-element.376), channel_id=1, source_target_pairs={{12,8},{8,4},{4,0},{13,9},{9,5},{5,1},{14,10},{10,6},{6,2},{15,11}... | collective-permute-start | bytes 786440 | tf_op jit(solution)/shard_map/ppermute | solution.py:262
  142.9 1.9 collective-permute-start.48
  144.9 2.2 collective-permute-done.46
  147.1 1.9 collective-permute-start.49
  149.4 3.4 %collective-permute-start.50 = (f16[1024,128]{1,0:T(8,128)(2,1)S(1)}, f16[1024,128]{1,0:T(8,128)(2,1)S(1)}, u32[]{:S(2)}, u32[]{:S(2)}) collective-permute-start(f16[1024,128]{1,0:T(8,128)(2,1)S(1)} %get-tuple-element.358), channel_id=1, source_target_pairs={{0,4},{4,8},{8,12},{1,5},{5,9},{9,13},{2,6},{6,10},{10,14},{3,7},{... | collective-permute-start | bytes 786440 | tf_op jit(solution)/shard_map/ppermute | solution.py:261
  152.8 1.9 collective-permute-start.51
  156.6 3.6 %collective-permute-start.52 = (f16[1024,128]{1,0:T(8,128)(2,1)S(1)}, f16[1024,128]{1,0:T(8,128)(2,1)S(1)}, u32[]{:S(2)}, u32[]{:S(2)}) collective-permute-start(f16[1024,128]{1,0:T(8,128)(2,1)S(1)} %get-tuple-element.361), channel_id=1, source_target_pairs={{0,4},{4,8},{8,12},{1,5},{5,9},{9,13},{2,6},{6,10},{10,14},{3,7},{... | collective-permute-start | bytes 786440 | tf_op jit(solution)/shard_map/ppermute | solution.py:261
  160.2 1.9 collective-permute-start.53
  162.9 2.9 %fusion.2 = bf16[1024,128]{0,1:T(8,128)(2,1)S(1)} fusion(bf16[4096,128]{1,0:T(8,128)(2,1)S(1)} %multiply_convert_fusion.2, bf16[1024,4096]{1,0:T(8,128)(2,1)S(1)} %bitcast.146), kind=kOutput, calls=%fused_computation.23 | convolution fusion | flops 1073872896 | bytes 9699328 | tf_op jit(solution)/shard_map/dot_general | solution.py:359
  165.9 1.9 collective-permute-start.61
  167.8 2.1 collective-permute-start.54
  169.9 3.1 %collective-permute-start.55 = (f16[1024,128]{1,0:T(8,128)(2,1)S(1)}, f16[1024,128]{1,0:T(8,128)(2,1)S(1)}, u32[]{:S(2)}, u32[]{:S(2)}) collective-permute-start(f16[1024,128]{1,0:T(8,128)(2,1)S(1)} %get-tuple-element.364), channel_id=1, source_target_pairs={{12,8},{8,4},{4,0},{13,9},{9,5},{5,1},{14,10},{10,6},{6,2},{15,11}... | collective-permute-start | bytes 786440 | tf_op jit(solution)/shard_map/ppermute | solution.py:262
  173.5 2.1 collective-permute-start.56
  175.6 2.0 collective-permute-done.54
  177.6 1.9 collective-permute-start.57
  179.9 3.4 %collective-permute-start.58 = (f16[1024,128]{1,0:T(8,128)(2,1)S(1)}, f16[1024,128]{1,0:T(8,128)(2,1)S(1)}, u32[]{:S(2)}, u32[]{:S(2)}) collective-permute-start(f16[1024,128]{1,0:T(8,128)(2,1)S(1)} %get-tuple-element.346), channel_id=1, source_target_pairs={{0,4},{4,8},{8,12},{1,5},{5,9},{9,13},{2,6},{6,10},{10,14},{3,7},{... | collective-permute-start | bytes 786440 | tf_op jit(solution)/shard_map/ppermute | solution.py:261
  183.3 1.9 collective-permute-start.59
  187.3 3.4 %collective-permute-start.69 = (f16[1024,128]{1,0:T(8,128)(2,1)S(1)}, f16[1024,128]{1,0:T(8,128)(2,1)S(1)}, u32[]{:S(2)}, u32[]{:S(2)}) collective-permute-start(f16[1024,128]{1,0:T(8,128)(2,1)S(1)} %get-tuple-element.349), channel_id=1, source_target_pairs={{4,8},{8,12},{5,9},{9,13},{6,10},{10,14},{7,11},{11,15},{20,24},{2... | collective-permute-start | bytes 786440 | tf_op jit(solution)/shard_map/ppermute | solution.py:261
  190.7 2.1 collective-permute-start.70
  193.6 2.9 %fusion.3 = bf16[1024,128]{0,1:T(8,128)(2,1)S(1)} fusion(bf16[4096,128]{1,0:T(8,128)(2,1)S(1)} %multiply_convert_fusion.1, bf16[1024,4096]{1,0:T(8,128)(2,1)S(1)} %bitcast.146), kind=kOutput, calls=%fused_computation.24 | convolution fusion | flops 1073872896 | bytes 9699328 | tf_op jit(solution)/shard_map/dot_general | solution.py:359
  196.5 1.7 collective-permute-start.65
  199.5 3.0 %collective-permute-start.71 = (f16[1024,128]{1,0:T(8,128)(2,1)S(1)}, f16[1024,128]{1,0:T(8,128)(2,1)S(1)}, u32[]{:S(2)}, u32[]{:S(2)}) collective-permute-start(f16[1024,128]{1,0:T(8,128)(2,1)S(1)} %get-tuple-element.351), channel_id=1, source_target_pairs={{4,8},{8,12},{5,9},{9,13},{6,10},{10,14},{7,11},{11,15},{20,24},{2... | collective-permute-start | bytes 786440 | tf_op jit(solution)/shard_map/ppermute | solution.py:261
  203.1 1.9 collective-permute-start.72
  206.0 2.1 collective-permute-done.71
  209.5 3.1 %collective-permute-done.72 = f16[1024,128]{1,0:T(8,128)(2,1)S(1)} collective-permute-done((f16[1024,128]{1,0:T(8,128)(2,1)S(1)}, f16[1024,128]{1,0:T(8,128)(2,1)S(1)}, u32[]{:S(2)}, u32[]{:S(2)}) %collective-permute-start.72) | collective-permute-done | bytes 262176 | tf_op jit(solution)/shard_map/ppermute | solution.py:262
  213.6 2.3 collective-permute-start.76
  222.2 1.8 collective-permute-start.79
  224.0 4.3 %collective-permute-done.77 = bf16[384,384]{0,1:T(8,128)(2,1)S(1)} collective-permute-done((bf16[384,384]{0,1:T(8,128)(2,1)S(1)}, bf16[384,384]{0,1:T(8,128)(2,1)S(1)}, u32[]{:S(2)}, u32[]{:S(2)}) %collective-permute-start.77) | collective-permute-done | bytes 294944 | tf_op jit(solution)/shard_map/ppermute | solution.py:350
  228.3 2.9 %convolution_convert_fusion = bf16[128,1024]{1,0:T(8,128)(2,1)S(1)} fusion(bf16[4096,128]{1,0:T(8,128)(2,1)S(1)} %multiply_convert_fusion, bf16[1024,4096]{1,0:T(8,128)(2,1)S(1)} %bitcast.146), kind=kOutput, calls=%fused_computation.14 | convolution fusion | flops 1073872896 | bytes 9699328 | tf_op jit(solution)/shard_map/dot_general | solution.py:359
  232.7 4.8 %collective-permute-start.83 = (bf16[1024,128]{0,1:T(8,128)(2,1)S(1)}, bf16[1024,128]{0,1:T(8,128)(2,1)S(1)}, u32[]{:S(2)}, u32[]{:S(2)}) collective-permute-start(bf16[1024,128]{0,1:T(8,128)(2,1)S(1)} %bitcast.147), channel_id=1, source_target_pairs={{0,1},{1,0},{2,3},{3,2},{4,5},{5,4},{6,7},{7,6},{8,9},{9,8},{10,11... | collective-permute-start | bytes 786440 | tf_op jit(solution)/shard_map/ppermute | solution.py:28
  238.8 6.8 %collective-permute-done.78 = bf16[384,384]{0,1:T(8,128)(2,1)S(1)} collective-permute-done((bf16[384,384]{0,1:T(8,128)(2,1)S(1)}, bf16[384,384]{0,1:T(8,128)(2,1)S(1)}, u32[]{:S(2)}, u32[]{:S(2)}) %collective-permute-start.78) | collective-permute-done | bytes 294944 | tf_op jit(solution)/shard_map/ppermute | solution.py:350
  245.7 3.1 %collective-permute-start.81 = (bf16[384,128]{0,1:T(8,128)(2,1)S(1)}, bf16[384,128]{0,1:T(8,128)(2,1)S(1)}, u32[]{:S(2)}, u32[]{:S(2)}) collective-permute-start(bf16[384,128]{0,1:T(8,128)(2,1)S(1)} %get-tuple-element.403), channel_id=1, source_target_pairs={{0,8},{4,12},{8,0},{12,4},{1,9},{5,13},{9,1},{13,5},{2,10},{6,14},... | collective-permute-start | bytes 294920 | tf_op jit(solution)/shard_map/ppermute | solution.py:350
  249.4 4.4 %collective-permute-start.85 = (bf16[1024,128]{0,1:T(8,128)(2,1)S(1)}, bf16[1024,128]{0,1:T(8,128)(2,1)S(1)}, u32[]{:S(2)}, u32[]{:S(2)}) collective-permute-start(bf16[1024,128]{0,1:T(8,128)(2,1)S(1)} %collective-permute-done.84), channel_id=1, source_target_pairs={{0,1},{1,0},{2,3},{3,2},{4,5},{5,4},{6,7},{7,6},{8,9},{9,8},{10,11... | collective-permute-start | bytes 786440 | tf_op jit(solution)/shard_map/ppermute | solution.py:28
  255.5 1.8 collective-permute-start.86
  260.3 8.0 %collective-permute-done.87 = bf16[128,512]{0,1:T(8,128)(2,1)S(1)} collective-permute-done((bf16[128,512]{0,1:T(8,128)(2,1)S(1)}, bf16[128,512]{0,1:T(8,128)(2,1)S(1)}, u32[]{:S(2)}, u32[]{:S(2)}) %collective-permute-start.87) | collective-permute-done | bytes 131104 | tf_op jit(solution)/shard_map/ppermute | solution.py:350
  268.2 1.7 collective-permute-done.88
  (186 shorter events, 64.7 us)
Async XLA Ops:
  5.2 16.8 %collective-permute-start.12 = (bf16[7,128,128]{2,1,0:T(8,128)(2,1)S(1)}, bf16[7,128,128]{2,1,0:T(8,128)(2,1)S(1)}, u32[]{:S(2)}, u32[]{:S(2)}) collective-permute-start(bf16[7,128,128]{2,1,0:T(8,128)(2,1)S(1)} %get-tuple-element.258), channel_id=1, source_target_pairs={{0,4},{4,8},{8,12},{12,0},{1,5},{5,9},{9,13},{13,1},{2,6},{6,10},{... | collective-permute-start | bytes 688136 | tf_op jit(solution)/shard_map/ppermute | solution.py:297
  6.6 19.0 %collective-permute-start.13 = (bf16[7,128,128]{2,1,0:T(8,128)(2,1)S(1)}, bf16[7,128,128]{2,1,0:T(8,128)(2,1)S(1)}, u32[]{:S(2)}, u32[]{:S(2)}) collective-permute-start(bf16[7,128,128]{2,1,0:T(8,128)(2,1)S(1)} %get-tuple-element.259), channel_id=1, source_target_pairs={{0,8},{4,12},{8,0},{12,4},{1,9},{5,13},{9,1},{13,5},{2,10},{6,14},... | collective-permute-start | bytes 688136 | tf_op jit(solution)/shard_map/ppermute | solution.py:297
  7.7 20.8 %collective-permute-start.14 = (bf16[7,128,128]{2,1,0:T(8,128)(2,1)S(1)}, bf16[7,128,128]{2,1,0:T(8,128)(2,1)S(1)}, u32[]{:S(2)}, u32[]{:S(2)}) collective-permute-start(bf16[7,128,128]{2,1,0:T(8,128)(2,1)S(1)} %get-tuple-element.260), channel_id=1, source_target_pairs={{0,12},{4,0},{8,4},{12,8},{1,13},{5,1},{9,5},{13,9},{2,14},{6,2},{... | collective-permute-start | bytes 688136 | tf_op jit(solution)/shard_map/ppermute | solution.py:297
  31.4 17.1 %collective-permute-start.19 = (bf16[7,128,128]{2,1,0:T(8,128)(2,1)S(1)}, bf16[7,128,128]{2,1,0:T(8,128)(2,1)S(1)}, u32[]{:S(2)}, u32[]{:S(2)}) collective-permute-start(bf16[7,128,128]{2,1,0:T(8,128)(2,1)S(1)} %collective-permute-done.12.refs_0_), channel_id=1, source_target_pairs={{0,2},{1,3},{2,0},{3,1},{4,6},{5,7},{6,4},{7,5},{8,10},{9,11},{10,... | collective-permute-start | bytes 688136 | tf_op jit(solution)/shard_map/ppermute | solution.py:28
  32.7 15.8 %collective-permute-start.20 = (bf16[7,128,128]{2,1,0:T(8,128)(2,1)S(1)}, bf16[7,128,128]{2,1,0:T(8,128)(2,1)S(1)}, u32[]{:S(2)}, u32[]{:S(2)}) collective-permute-start(bf16[7,128,128]{2,1,0:T(8,128)(2,1)S(1)} %collective-permute-done.13.refs_1_), channel_id=1, source_target_pairs={{0,2},{1,3},{2,0},{3,1},{4,6},{5,7},{6,4},{7,5},{8,10},{9,11},{10,... | collective-permute-start | bytes 688136 | tf_op jit(solution)/shard_map/ppermute | solution.py:28
  33.0 16.0 %collective-permute-start.21 = (bf16[7,128,128]{2,1,0:T(8,128)(2,1)S(1)}, bf16[7,128,128]{2,1,0:T(8,128)(2,1)S(1)}, u32[]{:S(2)}, u32[]{:S(2)}) collective-permute-start(bf16[7,128,128]{2,1,0:T(8,128)(2,1)S(1)} %collective-permute-done.14.refs_2_), channel_id=1, source_target_pairs={{0,2},{1,3},{2,0},{3,1},{4,6},{5,7},{6,4},{7,5},{8,10},{9,11},{10,... | collective-permute-start | bytes 688136 | tf_op jit(solution)/shard_map/ppermute | solution.py:28
  34.2 15.2 %collective-permute-start.16 = (bf16[7,128,128]{2,1,0:T(8,128)(2,1)S(1)}, bf16[7,128,128]{2,1,0:T(8,128)(2,1)S(1)}, u32[]{:S(2)}, u32[]{:S(2)}) collective-permute-start(bf16[7,128,128]{2,1,0:T(8,128)(2,1)S(1)} %collective-permute-done.12.refs_0_), channel_id=1, source_target_pairs={{0,1},{1,0},{2,3},{3,2},{4,5},{5,4},{6,7},{7,6},{8,9},{9,8},{10,11... | collective-permute-start | bytes 688136 | tf_op jit(solution)/shard_map/ppermute | solution.py:28
  68.8 9.5 %collective-permute-start.28 = (f16[1024,128]{1,0:T(8,128)(2,1)S(1)}, f16[1024,128]{1,0:T(8,128)(2,1)S(1)}, u32[]{:S(2)}, u32[]{:S(2)}) collective-permute-start(f16[1024,128]{1,0:T(8,128)(2,1)S(1)} %get-tuple-element.388), channel_id=1, source_target_pairs={{0,4},{1,5},{2,6},{3,7},{16,20},{17,21},{18,22},{19,23}} | collective-permute-start | bytes 786440 | tf_op jit(solution)/shard_map/ppermute | solution.py:261
  70.1 8.2 %collective-permute-start.29 = (f16[1024,128]{1,0:T(8,128)(2,1)S(1)}, f16[1024,128]{1,0:T(8,128)(2,1)S(1)}, u32[]{:S(2)}, u32[]{:S(2)}) collective-permute-start(f16[1024,128]{1,0:T(8,128)(2,1)S(1)} %get-tuple-element.391), channel_id=1, source_target_pairs={{12,8},{13,9},{14,10},{15,11},{28,24},{29,25},{30,26},{31,27}} | collective-permute-start | bytes 786440 | tf_op jit(solution)/shard_map/ppermute | solution.py:262
  70.9 15.0 %collective-permute-start.32 = (f16[1024,128]{1,0:T(8,128)(2,1)S(1)}, f16[1024,128]{1,0:T(8,128)(2,1)S(1)}, u32[]{:S(2)}, u32[]{:S(2)}) collective-permute-start(f16[1024,128]{1,0:T(8,128)(2,1)S(1)} %get-tuple-element.390), channel_id=1, source_target_pairs={{0,4},{1,5},{2,6},{3,7},{16,20},{17,21},{18,22},{19,23}} | collective-permute-start | bytes 786440 | tf_op jit(solution)/shard_map/ppermute | solution.py:261
  72.2 13.7 %collective-permute-start.33 = (f16[1024,128]{1,0:T(8,128)(2,1)S(1)}, f16[1024,128]{1,0:T(8,128)(2,1)S(1)}, u32[]{:S(2)}, u32[]{:S(2)}) collective-permute-start(f16[1024,128]{1,0:T(8,128)(2,1)S(1)} %get-tuple-element.389), channel_id=1, source_target_pairs={{12,8},{13,9},{14,10},{15,11},{28,24},{29,25},{30,26},{31,27}} | collective-permute-start | bytes 786440 | tf_op jit(solution)/shard_map/ppermute | solution.py:262
  79.9 12.8 %collective-permute-start.30 = (f16[1024,128]{1,0:T(8,128)(2,1)S(1)}, f16[1024,128]{1,0:T(8,128)(2,1)S(1)}, u32[]{:S(2)}, u32[]{:S(2)}) collective-permute-start(f16[1024,128]{1,0:T(8,128)(2,1)S(1)} %get-tuple-element.387), channel_id=1, source_target_pairs={{0,4},{4,8},{1,5},{5,9},{2,6},{6,10},{3,7},{7,11},{16,20},{20,24},... | collective-permute-start | bytes 786440 | tf_op jit(solution)/shard_map/ppermute | solution.py:261
  84.6 8.1 %collective-permute-start.31 = (f16[1024,128]{1,0:T(8,128)(2,1)S(1)}, f16[1024,128]{1,0:T(8,128)(2,1)S(1)}, u32[]{:S(2)}, u32[]{:S(2)}) collective-permute-start(f16[1024,128]{1,0:T(8,128)(2,1)S(1)} %get-tuple-element.386), channel_id=1, source_target_pairs={{12,8},{8,4},{13,9},{9,5},{14,10},{10,6},{15,11},{11,7},{28,24},{2... | collective-permute-start | bytes 786440 | tf_op jit(solution)/shard_map/ppermute | solution.py:262
  87.4 12.8 %collective-permute-start.36 = (f16[1024,128]{1,0:T(8,128)(2,1)S(1)}, f16[1024,128]{1,0:T(8,128)(2,1)S(1)}, u32[]{:S(2)}, u32[]{:S(2)}) collective-permute-start(f16[1024,128]{1,0:T(8,128)(2,1)S(1)} %get-tuple-element.385), channel_id=1, source_target_pairs={{0,4},{4,8},{1,5},{5,9},{2,6},{6,10},{3,7},{7,11},{16,20},{20,24},... | collective-permute-start | bytes 786440 | tf_op jit(solution)/shard_map/ppermute | solution.py:261
  91.4 8.8 %collective-permute-start.37 = (f16[1024,128]{1,0:T(8,128)(2,1)S(1)}, f16[1024,128]{1,0:T(8,128)(2,1)S(1)}, u32[]{:S(2)}, u32[]{:S(2)}) collective-permute-start(f16[1024,128]{1,0:T(8,128)(2,1)S(1)} %get-tuple-element.384), channel_id=1, source_target_pairs={{12,8},{8,4},{13,9},{9,5},{14,10},{10,6},{15,11},{11,7},{28,24},{2... | collective-permute-start | bytes 786440 | tf_op jit(solution)/shard_map/ppermute | solution.py:262
  94.3 12.9 %collective-permute-start.34 = (f16[1024,128]{1,0:T(8,128)(2,1)S(1)}, f16[1024,128]{1,0:T(8,128)(2,1)S(1)}, u32[]{:S(2)}, u32[]{:S(2)}) collective-permute-start(f16[1024,128]{1,0:T(8,128)(2,1)S(1)} %get-tuple-element.383), channel_id=1, source_target_pairs={{0,4},{4,8},{8,12},{1,5},{5,9},{9,13},{2,6},{6,10},{10,14},{3,7},{... | collective-permute-start | bytes 786440 | tf_op jit(solution)/shard_map/ppermute | solution.py:261
  98.3 9.0 %collective-permute-start.35 = (f16[1024,128]{1,0:T(8,128)(2,1)S(1)}, f16[1024,128]{1,0:T(8,128)(2,1)S(1)}, u32[]{:S(2)}, u32[]{:S(2)}) collective-permute-start(f16[1024,128]{1,0:T(8,128)(2,1)S(1)} %get-tuple-element.382), channel_id=1, source_target_pairs={{12,8},{8,4},{4,0},{13,9},{9,5},{5,1},{14,10},{10,6},{6,2},{15,11}... | collective-permute-start | bytes 786440 | tf_op jit(solution)/shard_map/ppermute | solution.py:262
  101.9 11.3 %collective-permute-start.38 = (f16[1024,128]{1,0:T(8,128)(2,1)S(1)}, f16[1024,128]{1,0:T(8,128)(2,1)S(1)}, u32[]{:S(2)}, u32[]{:S(2)}) collective-permute-start(f16[1024,128]{1,0:T(8,128)(2,1)S(1)} %get-tuple-element.380), channel_id=1, source_target_pairs={{0,4},{4,8},{8,12},{1,5},{5,9},{9,13},{2,6},{6,10},{10,14},{3,7},{... | collective-permute-start | bytes 786440 | tf_op jit(solution)/shard_map/ppermute | solution.py:261
  105.3 7.9 %collective-permute-start.39 = (f16[1024,128]{1,0:T(8,128)(2,1)S(1)}, f16[1024,128]{1,0:T(8,128)(2,1)S(1)}, u32[]{:S(2)}, u32[]{:S(2)}) collective-permute-start(f16[1024,128]{1,0:T(8,128)(2,1)S(1)} %get-tuple-element.381), channel_id=1, source_target_pairs={{12,8},{8,4},{4,0},{13,9},{9,5},{5,1},{14,10},{10,6},{6,2},{15,11}... | collective-permute-start | bytes 786440 | tf_op jit(solution)/shard_map/ppermute | solution.py:262
  107.6 11.3 %collective-permute-start.40 = (f16[1024,128]{1,0:T(8,128)(2,1)S(1)}, f16[1024,128]{1,0:T(8,128)(2,1)S(1)}, u32[]{:S(2)}, u32[]{:S(2)}) collective-permute-start(f16[1024,128]{1,0:T(8,128)(2,1)S(1)} %get-tuple-element.367), channel_id=1, source_target_pairs={{0,4},{4,8},{8,12},{1,5},{5,9},{9,13},{2,6},{6,10},{10,14},{3,7},{... | collective-permute-start | bytes 786440 | tf_op jit(solution)/shard_map/ppermute | solution.py:261
  111.0 8.2 %collective-permute-start.41 = (f16[1024,128]{1,0:T(8,128)(2,1)S(1)}, f16[1024,128]{1,0:T(8,128)(2,1)S(1)}, u32[]{:S(2)}, u32[]{:S(2)}) collective-permute-start(f16[1024,128]{1,0:T(8,128)(2,1)S(1)} %get-tuple-element.366), channel_id=1, source_target_pairs={{12,8},{8,4},{4,0},{13,9},{9,5},{5,1},{14,10},{10,6},{6,2},{15,11}... | collective-permute-start | bytes 786440 | tf_op jit(solution)/shard_map/ppermute | solution.py:262
  113.6 11.5 %collective-permute-start.42 = (f16[1024,128]{1,0:T(8,128)(2,1)S(1)}, f16[1024,128]{1,0:T(8,128)(2,1)S(1)}, u32[]{:S(2)}, u32[]{:S(2)}) collective-permute-start(f16[1024,128]{1,0:T(8,128)(2,1)S(1)} %get-tuple-element.370), channel_id=1, source_target_pairs={{0,4},{4,8},{8,12},{1,5},{5,9},{9,13},{2,6},{6,10},{10,14},{3,7},{... | collective-permute-start | bytes 786440 | tf_op jit(solution)/shard_map/ppermute | solution.py:261
  117.0 8.8 %collective-permute-start.43 = (f16[1024,128]{1,0:T(8,128)(2,1)S(1)}, f16[1024,128]{1,0:T(8,128)(2,1)S(1)}, u32[]{:S(2)}, u32[]{:S(2)}) collective-permute-start(f16[1024,128]{1,0:T(8,128)(2,1)S(1)} %get-tuple-element.369), channel_id=1, source_target_pairs={{12,8},{8,4},{4,0},{13,9},{9,5},{5,1},{14,10},{10,6},{6,2},{15,11}... | collective-permute-start | bytes 786440 | tf_op jit(solution)/shard_map/ppermute | solution.py:262
  119.6 19.6 %collective-permute-start.44 = (f16[1024,128]{1,0:T(8,128)(2,1)S(1)}, f16[1024,128]{1,0:T(8,128)(2,1)S(1)}, u32[]{:S(2)}, u32[]{:S(2)}) collective-permute-start(f16[1024,128]{1,0:T(8,128)(2,1)S(1)} %get-tuple-element.373), channel_id=1, source_target_pairs={{0,4},{4,8},{8,12},{1,5},{5,9},{9,13},{2,6},{6,10},{10,14},{3,7},{... | collective-permute-start | bytes 786440 | tf_op jit(solution)/shard_map/ppermute | solution.py:261
  122.7 19.9 %collective-permute-start.45 = (f16[1024,128]{1,0:T(8,128)(2,1)S(1)}, f16[1024,128]{1,0:T(8,128)(2,1)S(1)}, u32[]{:S(2)}, u32[]{:S(2)}) collective-permute-start(f16[1024,128]{1,0:T(8,128)(2,1)S(1)} %get-tuple-element.372), channel_id=1, source_target_pairs={{12,8},{8,4},{4,0},{13,9},{9,5},{5,1},{14,10},{10,6},{6,2},{15,11}... | collective-permute-start | bytes 786440 | tf_op jit(solution)/shard_map/ppermute | solution.py:262
  129.4 23.3 %collective-permute-start.63 = (bf16[1024,128]{0,1:T(8,128)(2,1)S(1)}, bf16[1024,128]{0,1:T(8,128)(2,1)S(1)}, u32[]{:S(2)}, u32[]{:S(2)}) collective-permute-start(bf16[1024,128]{0,1:T(8,128)(2,1)S(1)} %fusion.1), channel_id=1, source_target_pairs={{0,2},{1,3},{2,0},{3,1},{4,6},{5,7},{6,4},{7,5},{8,10},{9,11},{10,... | collective-permute-start | bytes 786440 | tf_op jit(solution)/shard_map/ppermute | solution.py:28
  130.4 24.3 %collective-permute-start.60 = (bf16[1024,128]{0,1:T(8,128)(2,1)S(1)}, bf16[1024,128]{0,1:T(8,128)(2,1)S(1)}, u32[]{:S(2)}, u32[]{:S(2)}) collective-permute-start(bf16[1024,128]{0,1:T(8,128)(2,1)S(1)} %fusion.1), channel_id=1, source_target_pairs={{0,1},{1,0},{2,3},{3,2},{4,5},{5,4},{6,7},{7,6},{8,9},{9,8},{10,11... | collective-permute-start | bytes 786440 | tf_op jit(solution)/shard_map/ppermute | solution.py:28
  137.3 9.8 %collective-permute-start.46 = (f16[1024,128]{1,0:T(8,128)(2,1)S(1)}, f16[1024,128]{1,0:T(8,128)(2,1)S(1)}, u32[]{:S(2)}, u32[]{:S(2)}) collective-permute-start(f16[1024,128]{1,0:T(8,128)(2,1)S(1)} %get-tuple-element.375), channel_id=1, source_target_pairs={{0,4},{4,8},{8,12},{1,5},{5,9},{9,13},{2,6},{6,10},{10,14},{3,7},{... | collective-permute-start | bytes 786440 | tf_op jit(solution)/shard_map/ppermute | solution.py:261
  139.2 9.8 %collective-permute-start.47 = (f16[1024,128]{1,0:T(8,128)(2,1)S(1)}, f16[1024,128]{1,0:T(8,128)(2,1)S(1)}, u32[]{:S(2)}, u32[]{:S(2)}) collective-permute-start(f16[1024,128]{1,0:T(8,128)(2,1)S(1)} %get-tuple-element.376), channel_id=1, source_target_pairs={{12,8},{8,4},{4,0},{13,9},{9,5},{5,1},{14,10},{10,6},{6,2},{15,11}... | collective-permute-start | bytes 786440 | tf_op jit(solution)/shard_map/ppermute | solution.py:262
  142.9 13.2 %collective-permute-start.48 = (f16[1024,128]{1,0:T(8,128)(2,1)S(1)}, f16[1024,128]{1,0:T(8,128)(2,1)S(1)}, u32[]{:S(2)}, u32[]{:S(2)}) collective-permute-start(f16[1024,128]{1,0:T(8,128)(2,1)S(1)} %get-tuple-element.355), channel_id=1, source_target_pairs={{0,4},{4,8},{8,12},{1,5},{5,9},{9,13},{2,6},{6,10},{10,14},{3,7},{... | collective-permute-start | bytes 786440 | tf_op jit(solution)/shard_map/ppermute | solution.py:261
  147.1 9.1 %collective-permute-start.49 = (f16[1024,128]{1,0:T(8,128)(2,1)S(1)}, f16[1024,128]{1,0:T(8,128)(2,1)S(1)}, u32[]{:S(2)}, u32[]{:S(2)}) collective-permute-start(f16[1024,128]{1,0:T(8,128)(2,1)S(1)} %get-tuple-element.354), channel_id=1, source_target_pairs={{12,8},{8,4},{4,0},{13,9},{9,5},{5,1},{14,10},{10,6},{6,2},{15,11}... | collective-permute-start | bytes 786440 | tf_op jit(solution)/shard_map/ppermute | solution.py:262
  149.4 12.8 %collective-permute-start.50 = (f16[1024,128]{1,0:T(8,128)(2,1)S(1)}, f16[1024,128]{1,0:T(8,128)(2,1)S(1)}, u32[]{:S(2)}, u32[]{:S(2)}) collective-permute-start(f16[1024,128]{1,0:T(8,128)(2,1)S(1)} %get-tuple-element.358), channel_id=1, source_target_pairs={{0,4},{4,8},{8,12},{1,5},{5,9},{9,13},{2,6},{6,10},{10,14},{3,7},{... | collective-permute-start | bytes 786440 | tf_op jit(solution)/shard_map/ppermute | solution.py:261
  152.8 9.4 %collective-permute-start.51 = (f16[1024,128]{1,0:T(8,128)(2,1)S(1)}, f16[1024,128]{1,0:T(8,128)(2,1)S(1)}, u32[]{:S(2)}, u32[]{:S(2)}) collective-permute-start(f16[1024,128]{1,0:T(8,128)(2,1)S(1)} %get-tuple-element.357), channel_id=1, source_target_pairs={{12,8},{8,4},{4,0},{13,9},{9,5},{5,1},{14,10},{10,6},{6,2},{15,11}... | collective-permute-start | bytes 786440 | tf_op jit(solution)/shard_map/ppermute | solution.py:262
  154.7 13.0 %collective-permute-start.66 = (bf16[1024,128]{0,1:T(8,128)(2,1)S(1)}, bf16[1024,128]{0,1:T(8,128)(2,1)S(1)}, u32[]{:S(2)}, u32[]{:S(2)}) collective-permute-start(bf16[1024,128]{0,1:T(8,128)(2,1)S(1)} %collective-permute-done.63), channel_id=1, source_target_pairs={{0,1},{1,0},{2,3},{3,2},{4,5},{5,4},{6,7},{7,6},{8,9},{9,8},{10,11... | collective-permute-start | bytes 786440 | tf_op jit(solution)/shard_map/ppermute | solution.py:28
  156.6 13.4 %collective-permute-start.52 = (f16[1024,128]{1,0:T(8,128)(2,1)S(1)}, f16[1024,128]{1,0:T(8,128)(2,1)S(1)}, u32[]{:S(2)}, u32[]{:S(2)}) collective-permute-start(f16[1024,128]{1,0:T(8,128)(2,1)S(1)} %get-tuple-element.361), channel_id=1, source_target_pairs={{0,4},{4,8},{8,12},{1,5},{5,9},{9,13},{2,6},{6,10},{10,14},{3,7},{... | collective-permute-start | bytes 786440 | tf_op jit(solution)/shard_map/ppermute | solution.py:261
  160.2 12.9 %collective-permute-start.53 = (f16[1024,128]{1,0:T(8,128)(2,1)S(1)}, f16[1024,128]{1,0:T(8,128)(2,1)S(1)}, u32[]{:S(2)}, u32[]{:S(2)}) collective-permute-start(f16[1024,128]{1,0:T(8,128)(2,1)S(1)} %get-tuple-element.360), channel_id=1, source_target_pairs={{12,8},{8,4},{4,0},{13,9},{9,5},{5,1},{14,10},{10,6},{6,2},{15,11}... | collective-permute-start | bytes 786440 | tf_op jit(solution)/shard_map/ppermute | solution.py:262
  165.8 17.5 %collective-permute-start.64 = (bf16[1024,128]{0,1:T(8,128)(2,1)S(1)}, bf16[1024,128]{0,1:T(8,128)(2,1)S(1)}, u32[]{:S(2)}, u32[]{:S(2)}) collective-permute-start(bf16[1024,128]{0,1:T(8,128)(2,1)S(1)} %fusion.2), channel_id=1, source_target_pairs={{0,2},{1,3},{2,0},{3,1},{4,6},{5,7},{6,4},{7,5},{8,10},{9,11},{10,... | collective-permute-start | bytes 786440 | tf_op jit(solution)/shard_map/ppermute | solution.py:28
  165.9 19.4 %collective-permute-start.61 = (bf16[1024,128]{0,1:T(8,128)(2,1)S(1)}, bf16[1024,128]{0,1:T(8,128)(2,1)S(1)}, u32[]{:S(2)}, u32[]{:S(2)}) collective-permute-start(bf16[1024,128]{0,1:T(8,128)(2,1)S(1)} %fusion.2), channel_id=1, source_target_pairs={{0,1},{1,0},{2,3},{3,2},{4,5},{5,4},{6,7},{7,6},{8,9},{9,8},{10,11... | collective-permute-start | bytes 786440 | tf_op jit(solution)/shard_map/ppermute | solution.py:28
  167.8 9.8 %collective-permute-start.54 = (f16[1024,128]{1,0:T(8,128)(2,1)S(1)}, f16[1024,128]{1,0:T(8,128)(2,1)S(1)}, u32[]{:S(2)}, u32[]{:S(2)}) collective-permute-start(f16[1024,128]{1,0:T(8,128)(2,1)S(1)} %get-tuple-element.363), channel_id=1, source_target_pairs={{0,4},{4,8},{8,12},{1,5},{5,9},{9,13},{2,6},{6,10},{10,14},{3,7},{... | collective-permute-start | bytes 786440 | tf_op jit(solution)/shard_map/ppermute | solution.py:261
  169.9 9.6 %collective-permute-start.55 = (f16[1024,128]{1,0:T(8,128)(2,1)S(1)}, f16[1024,128]{1,0:T(8,128)(2,1)S(1)}, u32[]{:S(2)}, u32[]{:S(2)}) collective-permute-start(f16[1024,128]{1,0:T(8,128)(2,1)S(1)} %get-tuple-element.364), channel_id=1, source_target_pairs={{12,8},{8,4},{4,0},{13,9},{9,5},{5,1},{14,10},{10,6},{6,2},{15,11}... | collective-permute-start | bytes 786440 | tf_op jit(solution)/shard_map/ppermute | solution.py:262
  173.5 13.5 %collective-permute-start.56 = (f16[1024,128]{1,0:T(8,128)(2,1)S(1)}, f16[1024,128]{1,0:T(8,128)(2,1)S(1)}, u32[]{:S(2)}, u32[]{:S(2)}) collective-permute-start(f16[1024,128]{1,0:T(8,128)(2,1)S(1)} %get-tuple-element.343), channel_id=1, source_target_pairs={{0,4},{4,8},{8,12},{1,5},{5,9},{9,13},{2,6},{6,10},{10,14},{3,7},{... | collective-permute-start | bytes 786440 | tf_op jit(solution)/shard_map/ppermute | solution.py:261
  177.6 9.4 %collective-permute-start.57 = (f16[1024,128]{1,0:T(8,128)(2,1)S(1)}, f16[1024,128]{1,0:T(8,128)(2,1)S(1)}, u32[]{:S(2)}, u32[]{:S(2)}) collective-permute-start(f16[1024,128]{1,0:T(8,128)(2,1)S(1)} %get-tuple-element.342), channel_id=1, source_target_pairs={{12,8},{8,4},{4,0},{13,9},{9,5},{5,1},{14,10},{10,6},{6,2},{15,11}... | collective-permute-start | bytes 786440 | tf_op jit(solution)/shard_map/ppermute | solution.py:262
  179.9 13.0 %collective-permute-start.58 = (f16[1024,128]{1,0:T(8,128)(2,1)S(1)}, f16[1024,128]{1,0:T(8,128)(2,1)S(1)}, u32[]{:S(2)}, u32[]{:S(2)}) collective-permute-start(f16[1024,128]{1,0:T(8,128)(2,1)S(1)} %get-tuple-element.346), channel_id=1, source_target_pairs={{0,4},{4,8},{8,12},{1,5},{5,9},{9,13},{2,6},{6,10},{10,14},{3,7},{... | collective-permute-start | bytes 786440 | tf_op jit(solution)/shard_map/ppermute | solution.py:261
  183.3 9.6 %collective-permute-start.59 = (f16[1024,128]{1,0:T(8,128)(2,1)S(1)}, f16[1024,128]{1,0:T(8,128)(2,1)S(1)}, u32[]{:S(2)}, u32[]{:S(2)}) collective-permute-start(f16[1024,128]{1,0:T(8,128)(2,1)S(1)} %get-tuple-element.345), channel_id=1, source_target_pairs={{12,8},{8,4},{4,0},{13,9},{9,5},{5,1},{14,10},{10,6},{6,2},{15,11}... | collective-permute-start | bytes 786440 | tf_op jit(solution)/shard_map/ppermute | solution.py:262
  185.2 14.3 %collective-permute-start.67 = (bf16[1024,128]{0,1:T(8,128)(2,1)S(1)}, bf16[1024,128]{0,1:T(8,128)(2,1)S(1)}, u32[]{:S(2)}, u32[]{:S(2)}) collective-permute-start(bf16[1024,128]{0,1:T(8,128)(2,1)S(1)} %collective-permute-done.64), channel_id=1, source_target_pairs={{0,1},{1,0},{2,3},{3,2},{4,5},{5,4},{6,7},{7,6},{8,9},{9,8},{10,11... | collective-permute-start | bytes 786440 | tf_op jit(solution)/shard_map/ppermute | solution.py:28
  187.3 15.8 %collective-permute-start.69 = (f16[1024,128]{1,0:T(8,128)(2,1)S(1)}, f16[1024,128]{1,0:T(8,128)(2,1)S(1)}, u32[]{:S(2)}, u32[]{:S(2)}) collective-permute-start(f16[1024,128]{1,0:T(8,128)(2,1)S(1)} %get-tuple-element.349), channel_id=1, source_target_pairs={{4,8},{8,12},{5,9},{9,13},{6,10},{10,14},{7,11},{11,15},{20,24},{2... | collective-permute-start | bytes 786440 | tf_op jit(solution)/shard_map/ppermute | solution.py:261
  190.7 14.3 %collective-permute-start.70 = (f16[1024,128]{1,0:T(8,128)(2,1)S(1)}, f16[1024,128]{1,0:T(8,128)(2,1)S(1)}, u32[]{:S(2)}, u32[]{:S(2)}) collective-permute-start(f16[1024,128]{1,0:T(8,128)(2,1)S(1)} %get-tuple-element.348), channel_id=1, source_target_pairs={{8,4},{4,0},{9,5},{5,1},{10,6},{6,2},{11,7},{7,3},{24,20},{20,16},... | collective-permute-start | bytes 786440 | tf_op jit(solution)/shard_map/ppermute | solution.py:262
  196.5 17.1 %collective-permute-start.65 = (bf16[1024,128]{0,1:T(8,128)(2,1)S(1)}, bf16[1024,128]{0,1:T(8,128)(2,1)S(1)}, u32[]{:S(2)}, u32[]{:S(2)}) collective-permute-start(bf16[1024,128]{0,1:T(8,128)(2,1)S(1)} %fusion.3), channel_id=1, source_target_pairs={{0,2},{1,3},{2,0},{3,1},{4,6},{5,7},{6,4},{7,5},{8,10},{9,11},{10,... | collective-permute-start | bytes 786440 | tf_op jit(solution)/shard_map/ppermute | solution.py:28
  198.2 18.3 %collective-permute-start.62 = (bf16[1024,128]{0,1:T(8,128)(2,1)S(1)}, bf16[1024,128]{0,1:T(8,128)(2,1)S(1)}, u32[]{:S(2)}, u32[]{:S(2)}) collective-permute-start(bf16[1024,128]{0,1:T(8,128)(2,1)S(1)} %fusion.3), channel_id=1, source_target_pairs={{0,1},{1,0},{2,3},{3,2},{4,5},{5,4},{6,7},{7,6},{8,9},{9,8},{10,11... | collective-permute-start | bytes 786440 | tf_op jit(solution)/shard_map/ppermute | solution.py:28
  199.5 8.7 %collective-permute-start.71 = (f16[1024,128]{1,0:T(8,128)(2,1)S(1)}, f16[1024,128]{1,0:T(8,128)(2,1)S(1)}, u32[]{:S(2)}, u32[]{:S(2)}) collective-permute-start(f16[1024,128]{1,0:T(8,128)(2,1)S(1)} %get-tuple-element.351), channel_id=1, source_target_pairs={{4,8},{8,12},{5,9},{9,13},{6,10},{10,14},{7,11},{11,15},{20,24},{2... | collective-permute-start | bytes 786440 | tf_op jit(solution)/shard_map/ppermute | solution.py:261
  203.1 9.5 %collective-permute-start.72 = (f16[1024,128]{1,0:T(8,128)(2,1)S(1)}, f16[1024,128]{1,0:T(8,128)(2,1)S(1)}, u32[]{:S(2)}, u32[]{:S(2)}) collective-permute-start(f16[1024,128]{1,0:T(8,128)(2,1)S(1)} %get-tuple-element.352), channel_id=1, source_target_pairs={{8,4},{4,0},{9,5},{5,1},{10,6},{6,2},{11,7},{7,3},{24,20},{20,16},... | collective-permute-start | bytes 786440 | tf_op jit(solution)/shard_map/ppermute | solution.py:262
  205.3 14.8 %collective-permute-start.73 = (f16[1024,128]{1,0:T(8,128)(2,1)S(1)}, f16[1024,128]{1,0:T(8,128)(2,1)S(1)}, u32[]{:S(2)}, u32[]{:S(2)}) collective-permute-start(f16[1024,128]{1,0:T(8,128)(2,1)S(1)} %get-tuple-element.334), channel_id=1, source_target_pairs={{8,12},{9,13},{10,14},{11,15},{24,28},{25,29},{26,30},{27,31}} | collective-permute-start | bytes 786440 | tf_op jit(solution)/shard_map/ppermute | solution.py:261
  208.2 12.0 %collective-permute-start.74 = (f16[1024,128]{1,0:T(8,128)(2,1)S(1)}, f16[1024,128]{1,0:T(8,128)(2,1)S(1)}, u32[]{:S(2)}, u32[]{:S(2)}) collective-permute-start(f16[1024,128]{1,0:T(8,128)(2,1)S(1)} %get-tuple-element.333), channel_id=1, source_target_pairs={{4,0},{5,1},{6,2},{7,3},{20,16},{21,17},{22,18},{23,19}} | collective-permute-start | bytes 786440 | tf_op jit(solution)/shard_map/ppermute | solution.py:262
  212.9 7.5 %collective-permute-start.75 = (f16[1024,128]{1,0:T(8,128)(2,1)S(1)}, f16[1024,128]{1,0:T(8,128)(2,1)S(1)}, u32[]{:S(2)}, u32[]{:S(2)}) collective-permute-start(f16[1024,128]{1,0:T(8,128)(2,1)S(1)} %get-tuple-element.337), channel_id=1, source_target_pairs={{8,12},{9,13},{10,14},{11,15},{24,28},{25,29},{26,30},{27,31}} | collective-permute-start | bytes 786440 | tf_op jit(solution)/shard_map/ppermute | solution.py:261
  220.1 8.3 %collective-permute-start.77 = (bf16[384,384]{0,1:T(8,128)(2,1)S(1)}, bf16[384,384]{0,1:T(8,128)(2,1)S(1)}, u32[]{:S(2)}, u32[]{:S(2)}) collective-permute-start(bf16[384,384]{0,1:T(8,128)(2,1)S(1)} %get-tuple-element.394), channel_id=1, source_target_pairs={{0,4},{4,8},{8,12},{12,0},{1,5},{5,9},{9,13},{13,1},{2,6},{6,10},{... | collective-permute-start | bytes 884744 | tf_op jit(solution)/shard_map/ppermute | solution.py:350
  221.7 24.0 %collective-permute-start.78 = (bf16[384,384]{0,1:T(8,128)(2,1)S(1)}, bf16[384,384]{0,1:T(8,128)(2,1)S(1)}, u32[]{:S(2)}, u32[]{:S(2)}) collective-permute-start(bf16[384,384]{0,1:T(8,128)(2,1)S(1)} %get-tuple-element.392), channel_id=1, source_target_pairs={{0,8},{4,12},{8,0},{12,4},{1,9},{5,13},{9,1},{13,5},{2,10},{6,14},... | collective-permute-start | bytes 884744 | tf_op jit(solution)/shard_map/ppermute | solution.py:350
  222.2 26.5 %collective-permute-start.79 = (bf16[384,384]{0,1:T(8,128)(2,1)S(1)}, bf16[384,384]{0,1:T(8,128)(2,1)S(1)}, u32[]{:S(2)}, u32[]{:S(2)}) collective-permute-start(bf16[384,384]{0,1:T(8,128)(2,1)S(1)} %get-tuple-element.393), channel_id=1, source_target_pairs={{0,12},{4,0},{8,4},{12,8},{1,13},{5,1},{9,5},{13,9},{2,14},{6,2},{... | collective-permute-start | bytes 884744 | tf_op jit(solution)/shard_map/ppermute | solution.py:350
  232.7 21.5 %collective-permute-start.83 = (bf16[1024,128]{0,1:T(8,128)(2,1)S(1)}, bf16[1024,128]{0,1:T(8,128)(2,1)S(1)}, u32[]{:S(2)}, u32[]{:S(2)}) collective-permute-start(bf16[1024,128]{0,1:T(8,128)(2,1)S(1)} %bitcast.147), channel_id=1, source_target_pairs={{0,1},{1,0},{2,3},{3,2},{4,5},{5,4},{6,7},{7,6},{8,9},{9,8},{10,11... | collective-permute-start | bytes 786440 | tf_op jit(solution)/shard_map/ppermute | solution.py:28
  237.5 11.8 %collective-permute-start.84 = (bf16[1024,128]{0,1:T(8,128)(2,1)S(1)}, bf16[1024,128]{0,1:T(8,128)(2,1)S(1)}, u32[]{:S(2)}, u32[]{:S(2)}) collective-permute-start(bf16[1024,128]{0,1:T(8,128)(2,1)S(1)} %bitcast.148), channel_id=1, source_target_pairs={{0,2},{1,3},{2,0},{3,1},{4,6},{5,7},{6,4},{7,5},{8,10},{9,11},{10,... | collective-permute-start | bytes 786440 | tf_op jit(solution)/shard_map/ppermute | solution.py:28
  237.6 19.9 %collective-permute-start.80 = (bf16[384,128]{0,1:T(8,128)(2,1)S(1)}, bf16[384,128]{0,1:T(8,128)(2,1)S(1)}, u32[]{:S(2)}, u32[]{:S(2)}) collective-permute-start(bf16[384,128]{0,1:T(8,128)(2,1)S(1)} %get-tuple-element.401), channel_id=1, source_target_pairs={{0,4},{4,8},{8,12},{12,0},{1,5},{5,9},{9,13},{13,1},{2,6},{6,10},{... | collective-permute-start | bytes 294920 | tf_op jit(solution)/shard_map/ppermute | solution.py:350
  245.7 12.9 %collective-permute-start.81 = (bf16[384,128]{0,1:T(8,128)(2,1)S(1)}, bf16[384,128]{0,1:T(8,128)(2,1)S(1)}, u32[]{:S(2)}, u32[]{:S(2)}) collective-permute-start(bf16[384,128]{0,1:T(8,128)(2,1)S(1)} %get-tuple-element.403), channel_id=1, source_target_pairs={{0,8},{4,12},{8,0},{12,4},{1,9},{5,13},{9,1},{13,5},{2,10},{6,14},... | collective-permute-start | bytes 294920 | tf_op jit(solution)/shard_map/ppermute | solution.py:350
  248.8 9.8 %collective-permute-start.82 = (bf16[384,128]{0,1:T(8,128)(2,1)S(1)}, bf16[384,128]{0,1:T(8,128)(2,1)S(1)}, u32[]{:S(2)}, u32[]{:S(2)}) collective-permute-start(bf16[384,128]{0,1:T(8,128)(2,1)S(1)} %get-tuple-element.402), channel_id=1, source_target_pairs={{0,12},{4,0},{8,4},{12,8},{1,13},{5,1},{9,5},{13,9},{2,14},{6,2},{... | collective-permute-start | bytes 294920 | tf_op jit(solution)/shard_map/ppermute | solution.py:350
  257.3 10.9 %collective-permute-start.87 = (bf16[128,512]{0,1:T(8,128)(2,1)S(1)}, bf16[128,512]{0,1:T(8,128)(2,1)S(1)}, u32[]{:S(2)}, u32[]{:S(2)}) collective-permute-start(bf16[128,512]{0,1:T(8,128)(2,1)S(1)} %get-tuple-element.400), channel_id=1, source_target_pairs={{0,8},{4,12},{8,0},{12,4},{1,9},{5,13},{9,1},{13,5},{2,10},{6,14},... | collective-permute-start | bytes 393224 | tf_op jit(solution)/shard_map/ppermute | solution.py:350
  257.6 12.4 %collective-permute-start.88 = (bf16[128,512]{0,1:T(8,128)(2,1)S(1)}, bf16[128,512]{0,1:T(8,128)(2,1)S(1)}, u32[]{:S(2)}, u32[]{:S(2)}) collective-permute-start(bf16[128,512]{0,1:T(8,128)(2,1)S(1)} %get-tuple-element.399), channel_id=1, source_target_pairs={{0,12},{4,0},{8,4},{12,8},{1,13},{5,1},{9,5},{13,9},{2,14},{6,2},{... | collective-permute-start | bytes 393224 | tf_op jit(solution)/shard_map/ppermute | solution.py:350
  (23 other events, 174.4 us)
